TPU v7x, 128 devices: a whole 4x4x4 slice. The times are simulated.
128 devices in a mesh: node: 8 (over x, core), local: 16 (over y, z).
Axes of the slice: x: 4, y: 4, z: 4, core: 2. Of those that a mesh axis runs over, the one named last changes fastest.
Arguments:
- tokens: bfloat16 [8192, 2048], P(('node', 'local')), may hold values from -6 to 6
- cotangent: bfloat16 [8192, 2048], P(('node', 'local')), may hold values from -6 to 6
- gate_weights: bfloat16 [8192, 6], P(('node', 'local')), may hold values from 0.099609375 to 1
- expert_ids: int32 [8192, 6], P(('node', 'local')), may hold values from 0 to 63, as said below
- gate_proj: bfloat16 [128, 2048, 704], P(('node', 'local')), may hold values from -0.125 to 0.125
- up_proj: bfloat16 [128, 2048, 704], P(('node', 'local')), may hold values from -0.125 to 0.125
- down_proj: bfloat16 [128, 704, 2048], P(('node', 'local')), may hold values from -0.15625 to 0.15625
Outputs:
- grad_tokens: bfloat16 [8192, 2048], P(('node', 'local'))
- grad_gates: float32 [8192, 6], P(('node', 'local'))
- grad_gate_proj: bfloat16 [128, 2048, 704], P(('node', 'local'))
- grad_up_proj: bfloat16 [128, 2048, 704], P(('node', 'local'))
- grad_down_proj: bfloat16 [128, 704, 2048], P(('node', 'local'))
Inputs may be any that keep to these rules, and one draw needn't show every extreme that they name: `expert_ids`: each row names 6 different experts, two in each of three different groups of 8 consecutive experts. The 64 rows of one device name one expert at most 9 times, and on every device some expert is named exactly 9 times.
All inputs are finite; a program needn't handle non-finite values.
Results may differ from a plain program's by a relative error of at most 0.0057.
Values may be sent and summed in bfloat16 or wider, within the bound.
No kernel may reach another device: no remote copies, remote signals or barrier semaphores. Data moves between devices by JAX's collectives and lax.ppermute only.
A program may use at most 128 MiB of HBM per device.

v0:
```python
import jax
import jax.numpy as jnp
from jax import lax
from jax.sharding import PartitionSpec as P

EXPERTS = 64
MOST = 9


def unit_pass(rows_x, rows_dy, rows_gate, gate_w, up_w, down_w):
    contract_cols = (((1,), (1,)), ((), ()))
    contract_rows = (((0,), (0,)), ((), ()))
    pre_gate = jnp.dot(rows_x, gate_w, preferred_element_type=jnp.float32)
    pre_up = jnp.dot(rows_x, up_w, preferred_element_type=jnp.float32)
    back_proj = lax.dot_general(rows_dy, down_w, contract_cols, preferred_element_type=jnp.float32)
    sigmoid_val = jax.nn.sigmoid(pre_gate)
    silu_val = pre_gate * sigmoid_val
    act = silu_val * pre_up
    gate_part = jnp.sum(act * back_proj, axis=1).astype(jnp.bfloat16)
    weight_col = rows_gate.astype(jnp.float32)[:, None]
    d_gate = (
        weight_col * back_proj * pre_up * sigmoid_val * (1.0 + pre_gate * (1.0 - sigmoid_val))
    ).astype(jnp.bfloat16)
    d_up = (weight_col * back_proj * silu_val).astype(jnp.bfloat16)
    scaled = (weight_col * act).astype(jnp.bfloat16)
    token_term = (
        lax.dot_general(d_gate, gate_w, contract_cols, preferred_element_type=jnp.float32)
        + lax.dot_general(d_up, up_w, contract_cols, preferred_element_type=jnp.float32)
    ).astype(jnp.bfloat16)
    grad_gate = lax.dot_general(
        rows_x, d_gate, contract_rows, preferred_element_type=jnp.float32
    ).astype(jnp.bfloat16)
    grad_up = lax.dot_general(
        rows_x, d_up, contract_rows, preferred_element_type=jnp.float32
    ).astype(jnp.bfloat16)
    grad_down = lax.dot_general(
        scaled, rows_dy, contract_rows, preferred_element_type=jnp.float32
    ).astype(jnp.bfloat16)
    return (token_term, gate_part, grad_gate, grad_up, grad_down)


def slot_numbers(id_rows, first_expert, expert_count, slot_depth):
    local_ids = id_rows - first_expert
    inside = (local_ids >= 0) & (local_ids < expert_count)
    hit_table = (
        (
            (local_ids[:, :, None] == jnp.arange(expert_count, dtype=jnp.int32)[None, None, :])
            & inside[:, :, None]
        )
        .astype(jnp.int32)
        .reshape(-1, expert_count)
    )
    rank_table = jnp.cumsum(hit_table, axis=0) - 1
    position = jnp.sum(rank_table * hit_table, axis=1).reshape(id_rows.shape)
    return jnp.where(inside, local_ids * slot_depth + position, -1)


def selectors(slot_of, slot_total):
    matches = slot_of[None, :, :] == jnp.arange(slot_total, dtype=jnp.int32)[:, None, None]
    select = jnp.any(matches, axis=2).astype(jnp.bfloat16)
    return (select, matches)


def spread_rows(rows, expert_count, slot_depth, halves):
    shaped = rows.reshape((expert_count, slot_depth) + rows.shape[1:])
    return jnp.repeat(shaped, halves, axis=0)


def pack_rows(
    source_x, source_dy, source_gate, id_rows, first_expert, expert_count, slot_depth, halves
):
    slot_of = slot_numbers(id_rows, first_expert, expert_count, slot_depth)
    select, matches = selectors(slot_of, expert_count * slot_depth)
    slot_gate = jnp.sum(
        jnp.where(matches, source_gate[None, :, :].astype(jnp.float32), 0.0), axis=(1, 2)
    )
    rows_x = jnp.dot(select, source_x, preferred_element_type=jnp.float32).astype(jnp.bfloat16)
    rows_dy = jnp.dot(select, source_dy, preferred_element_type=jnp.float32).astype(jnp.bfloat16)
    packed = (
        spread_rows(rows_x, expert_count, slot_depth, halves),
        spread_rows(rows_dy, expert_count, slot_depth, halves),
        spread_rows(slot_gate.astype(jnp.bfloat16), expert_count, slot_depth, halves),
    )
    return (packed, select, matches)


def expert_units(got_x, got_dy, got_gate, gate_proj, up_proj, down_proj):
    sources = got_x.shape[0]
    per_dev = gate_proj.shape[0]
    width = got_x.shape[2]
    shaped_x = got_x.reshape(sources, per_dev, -1, width)
    shaped_dy = got_dy.reshape(sources, per_dev, -1, width)
    shaped_gate = got_gate.reshape(sources, per_dev, -1)
    term_list, part_list, gate_list, up_list, down_list = ([], [], [], [], [])
    token_term, gate_part, grad_gate, grad_up, grad_down = unit_pass(
        shaped_x[:, 0].reshape(-1, width),
        shaped_dy[:, 0].reshape(-1, width),
        shaped_gate[:, 0].reshape(-1),
        gate_proj[0],
        up_proj[0],
        down_proj[0],
    )
    term_list.append(token_term.reshape(sources, -1, width))
    part_list.append(gate_part.reshape(sources, -1))
    gate_list.append(grad_gate)
    up_list.append(grad_up)
    down_list.append(grad_down)
    term_back = jnp.stack(term_list, axis=1).reshape(sources, -1, width)
    part_back = jnp.stack(part_list, axis=1).reshape(sources, -1)
    return (
        term_back,
        part_back,
        (jnp.stack(gate_list, 0), jnp.stack(up_list, 0), jnp.stack(down_list, 0)),
    )


def collect(back_terms, back_parts, select, matches, expert_count, halves):
    width = back_terms.shape[-1]
    shaped = back_terms.reshape(expert_count, halves, -1, width)
    part_sums = (
        back_parts.reshape(expert_count, halves, -1).astype(jnp.float32).sum(axis=1).reshape(-1)
    )
    total = None
    for half in range(halves):
        piece = lax.dot_general(
            select,
            shaped[:, half].reshape(-1, width),
            (((0,), (0,)), ((), ())),
            preferred_element_type=jnp.float32,
        )
        total = piece if total is None else total + piece
    gate_total = jnp.sum(jnp.where(matches, part_sums[:, None, None], 0.0), axis=0)
    return (total, gate_total)


def local(tokens, cotangent, gate_weights, expert_ids, gate_proj, up_proj, down_proj):
    node_count = lax.axis_size("node")
    local_count = lax.axis_size("local")
    devices = node_count * local_count
    halves = max(1, devices // EXPERTS)
    packed, select, matches = pack_rows(
        tokens, cotangent, gate_weights, expert_ids, 0, EXPERTS, MOST, halves
    )
    got_x, got_dy, got_gate = (
        lax.all_to_all(packed[0], ("node", "local"), split_axis=0, concat_axis=0, tiled=True),
        lax.all_to_all(packed[1], ("node", "local"), split_axis=0, concat_axis=0, tiled=True),
        lax.all_to_all(packed[2], ("node", "local"), split_axis=0, concat_axis=0, tiled=True),
    )
    term_back, part_back, grads = expert_units(
        got_x, got_dy, got_gate, gate_proj, up_proj, down_proj
    )
    ret_terms, ret_parts = (
        lax.all_to_all(term_back, ("node", "local"), split_axis=0, concat_axis=0, tiled=True),
        lax.all_to_all(part_back, ("node", "local"), split_axis=0, concat_axis=0, tiled=True),
    )
    row_total, grad_gates = collect(ret_terms, ret_parts, select, matches, EXPERTS, halves)
    grad_tokens = row_total.astype(jnp.bfloat16)
    return (grad_tokens, grad_gates, grads[0], grads[1], grads[2])


def solution(mesh):
    placed = (
        P(("node", "local"), None),
        P(("node", "local"), None),
        P(("node", "local"), None),
        P(("node", "local"), None),
        P(("node", "local"), None, None),
        P(("node", "local"), None, None),
        P(("node", "local"), None, None),
    )
    return jax.shard_map(
        local,
        mesh=mesh,
        in_specs=placed,
        out_specs=(
            P(("node", "local"), None),
            P(("node", "local"), None),
            P(("node", "local"), None, None),
            P(("node", "local"), None, None),
            P(("node", "local"), None, None),
        ),
        check_vma=False,
    )
```

profile of v0, /device:TPU:8, one launch (start us, length us, event | category | flops | bytes accessed | tf_op | source)
XLA Modules:
  0.0 475.5 jit_solution(5405201521169998106)
XLA Ops:
  5.4 3.2 convolution_convert_fusion.3
  8.6 4.6 reshape.97
  13.2 6.7 %broadcast_in_dim.49 = bf16[64,2,9,2048]{3,2,1,0:T(8,128)(2,1)} broadcast(bf16[64,9,2048]{2,1,0:T(8,128)(2,1)} %reshape.97), dimensions={0,2,3} | broadcast | bytes 7077888 | tf_op jit(solution)/shard_map/broadcast_in_dim | solution.py:66
  19.9 10.9 %all-to-all-start.2 = ((bf16[128,9,2048]{2,1,0:T(8,128)(2,1)}), bf16[128,9,2048]{2,1,0:T(8,128)(2,1)}, u32[]{:S(2)}, u32[]{:S(2)}) async-start(bf16[128,9,2048]{2,1,0:T(8,128)(2,1)} %bitcast.69), calls=%async_computation.2 | async-start | bytes 16777216 | tf_op jit(solution)/shard_map/all_to_all | solution.py:145
  30.9 2.2 convolution_convert_fusion.4
  33.1 4.6 reshape.95
  37.7 102.5 %all-to-all-done.2 = bf16[128,9,2048]{2,1,0:T(8,128)(2,1)} async-done(((bf16[128,9,2048]{2,1,0:T(8,128)(2,1)}), bf16[128,9,2048]{2,1,0:T(8,128)(2,1)}, u32[]{:S(2)}, u32[]{:S(2)}) %all-to-all-start.2) | async-done | bytes 4718624 | tf_op jit(solution)/shard_map/all_to_all | solution.py:145
  140.1 6.8 %broadcast_in_dim.48 = bf16[64,2,9,2048]{3,2,1,0:T(8,128)(2,1)} broadcast(bf16[64,9,2048]{2,1,0:T(8,128)(2,1)} %reshape.95), dimensions={0,2,3} | broadcast | bytes 7077888 | tf_op jit(solution)/shard_map/broadcast_in_dim | solution.py:66
  147.0 7.8 %all-to-all-start.1 = ((bf16[128,9,2048]{2,1,0:T(8,128)(2,1)}), bf16[128,9,2048]{2,1,0:T(8,128)(2,1)}, u32[]{:S(2)}, u32[]{:S(2)}) async-start(bf16[128,9,2048]{2,1,0:T(8,128)(2,1)} %bitcast.68), calls=%async_computation.1 | async-start | bytes 16777216 | tf_op jit(solution)/shard_map/all_to_all | solution.py:146
  154.8 8.5 %reshape_squeeze_reshape.8 = bf16[1152,2048]{1,0:T(8,128)(2,1)} reshape(bf16[128,9,2048]{2,1,0:T(8,128)(2,1)} %all-to-all-done.2) | data formatting | bytes 9437184 | tf_op jit(solution)/shard_map/reshape;squeeze;reshape | solution.py:96
  163.4 8.2 %fusion.6 = f32[1152,704]{0,1:T(8,128)} fusion(bf16[1152,2048]{1,0:T(8,128)(2,1)} %reshape_squeeze_reshape.8, bf16[1,2048,704]{1,2,0:T(8,128)(2,1)S(1)} %copy-done), kind=kOutput, calls=%fused_computation.19 | convolution fusion | flops 3321888768 | bytes 10846208 | tf_op jit(solution)/shard_map/dot_general | solution.py:13
  171.5 5.6 %fusion.9 = f32[1152,704]{0,1:T(8,128)} fusion(bf16[1152,2048]{1,0:T(8,128)(2,1)S(1)} %copy-done.3, bf16[1,2048,704]{1,2,0:T(8,128)(2,1)S(1)} %copy-done.11), kind=kOutput, calls=%fused_computation.22 | convolution fusion | flops 3321888768 | bytes 10846208 | tf_op jit(solution)/shard_map/dot_general | solution.py:14
  177.1 87.0 %all-to-all-done.1 = bf16[128,9,2048]{2,1,0:T(8,128)(2,1)} async-done(((bf16[128,9,2048]{2,1,0:T(8,128)(2,1)}), bf16[128,9,2048]{2,1,0:T(8,128)(2,1)}, u32[]{:S(2)}, u32[]{:S(2)}) %all-to-all-start.1) | async-done | bytes 4718624 | tf_op jit(solution)/shard_map/all_to_all | solution.py:146
  264.1 8.5 %reshape_squeeze_reshape.7 = bf16[1152,2048]{1,0:T(8,128)(2,1)} reshape(bf16[128,9,2048]{2,1,0:T(8,128)(2,1)} %all-to-all-done.1) | data formatting | bytes 9437184 | tf_op jit(solution)/shard_map/reshape;squeeze;reshape | solution.py:97
  272.7 10.8 %multiply_reduce_fusion = (bf16[1152]{0:T(1024)(128)(2,1)S(1)}, f32[1152,704]{0,1:T(8,128)}) fusion(f32[1152,704]{0,1:T(8,128)} %fusion.9, f32[1152,704]{0,1:T(8,128)} %fusion.6, bf16[1152,2048]{1,0:T(8,128)(2,1)} %reshape_squeeze_reshape.7, bf16[1,704,2048]{2,1,0:T(8,128)(2,1)} %param.13), kind=kOutput, calls=%fused_computation.7 | convolution fusion | flops 3327564800 | bytes 17336576 | tf_op jit(solution)/shard_map/dot_general | solution.py:15
  284.3 8.9 %all-to-all-start.4 = ((bf16[128,1,9]{2,1,0:T(2,128)(2,1)}), bf16[128,1,9]{2,1,0:T(2,128)(2,1)S(1)}, u32[]{:S(2)}, u32[]{:S(2)}) async-start(bf16[128,1,9]{2,1,0:T(2,128)(2,1)} %convert_element_type.103), calls=%async_computation.4 | async-start | bytes 131072 | tf_op jit(solution)/shard_map/all_to_all | solution.py:154
  293.3 9.1 %all-to-all-done.4 = bf16[128,1,9]{2,1,0:T(2,128)(2,1)S(1)} async-done(((bf16[128,1,9]{2,1,0:T(2,128)(2,1)}), bf16[128,1,9]{2,1,0:T(2,128)(2,1)S(1)}, u32[]{:S(2)}, u32[]{:S(2)}) %all-to-all-start.4) | async-done | bytes 2336 | tf_op jit(solution)/shard_map/all_to_all | solution.py:154
  303.9 13.9 %all_to_all.30 = bf16[128,1,9]{2,1,0:T(2,128)(2,1)S(1)} all-to-all(bf16[128,1,9]{2,1,0:T(2,128)(2,1)S(1)} %copy.73), channel_id=1, replica_groups=mesh['node'=8,'local'=16] {'node','local'}, dimensions={0} | all-to-all | bytes 4608 | tf_op jit(solution)/shard_map/all_to_all | solution.py:147
  318.2 4.7 multiply_convert_fusion.1
  322.9 3.9 fusion.4
  326.8 5.5 %add_convert_fusion = bf16[1152,2048]{1,0:T(8,128)(2,1)} fusion(f32[1152,2048]{1,0:T(8,128)S(1)} %fusion.4, bf16[1152,704]{0,1:T(8,128)(2,1)S(1)} %get-tuple-element.9, bf16[1,2048,704]{1,2,0:T(8,128)(2,1)S(1)} %copy-done.12), kind=kOutput, calls=%fused_computation | convolution fusion | flops 3326607360 | bytes 18661376 | tf_op jit(solution)/shard_map/dot_general | solution.py:28
  332.3 8.1 %reshape_stack_reshape.4 = bf16[128,9,2048]{2,1,0:T(8,128)(2,1)} reshape(bf16[1152,2048]{1,0:T(8,128)(2,1)} %add_convert_fusion) | data formatting | bytes 9437184 | tf_op jit(solution)/shard_map/reshape;stack;reshape | solution.py:108
  340.4 6.2 %all-to-all-start.3 = ((bf16[128,9,2048]{2,1,0:T(8,128)(2,1)}), bf16[128,9,2048]{2,1,0:T(8,128)(2,1)}, u32[]{:S(2)}, u32[]{:S(2)}) async-start(bf16[128,9,2048]{2,1,0:T(8,128)(2,1)} %reshape_stack_reshape.4), calls=%async_computation.3 | async-start | bytes 16777216 | tf_op jit(solution)/shard_map/all_to_all | solution.py:153
  346.7 8.4 %fusion.3 = bf16[1,2048,704]{1,2,0:T(8,128)(2,1)} fusion(bf16[1152,704]{0,1:T(8,128)(2,1)} %copy-done.8, bf16[1152,2048]{1,0:T(8,128)(2,1)} %reshape_squeeze_reshape.8), kind=kOutput, calls=%fused_computation.16 | convolution fusion | flops 3323330560 | bytes 9224192 | tf_op jit(solution)/shard_map/dot_general | solution.py:33
  355.2 5.2 %fusion.2 = bf16[1,2048,704]{1,2,0:T(8,128)(2,1)} fusion(bf16[1152,704]{0,1:T(8,128)(2,1)S(1)} %copy-done.7, bf16[1152,2048]{1,0:T(8,128)(2,1)S(1)} %bitcast.71), kind=kOutput, calls=%fused_computation.15 | convolution fusion | flops 3323330560 | bytes 9224192 | tf_op jit(solution)/shard_map/dot_general | solution.py:30
  360.4 5.4 %fusion.1 = bf16[1,704,2048]{2,1,0:T(8,128)(2,1)} fusion(bf16[1152,2048]{1,0:T(8,128)(2,1)S(1)} %bitcast.73, f32[1152]{0:T(1024)S(1)} %reshape.100, f32[1152,704]{0,1:T(8,128)S(1)} %copy-done.5, f32[1152,704]{0,1:T(8,128)S(1)} %copy-done.4), kind=kOutput, calls=%fused_computation.14 | convolution fusion | flops 3329007616 | bytes 14094848 | tf_op jit(solution)/shard_map/dot_general | solution.py:36
  365.8 90.2 %all-to-all-done.3 = bf16[128,9,2048]{2,1,0:T(8,128)(2,1)} async-done(((bf16[128,9,2048]{2,1,0:T(8,128)(2,1)}), bf16[128,9,2048]{2,1,0:T(8,128)(2,1)}, u32[]{:S(2)}, u32[]{:S(2)}) %all-to-all-start.3) | async-done | bytes 4718624 | tf_op jit(solution)/shard_map/all_to_all | solution.py:153
  456.1 6.2 %slice_bitcast_fusion = (bf16[64,1,9,2048]{3,2,0,1:T(8,128)(2,1)}, bf16[64,1,9,2048]{3,2,0,1:T(8,128)(2,1)}) fusion(bf16[64,2,9,2048]{3,2,1,0:T(8,128)(2,1)} %bitcast.7), kind=kLoop, calls=%fused_computation.1 | loop fusion | bytes 9437184
  462.2 4.7 reshape_squeeze.7
  466.9 4.9 %reshape_squeeze.6 = bf16[576,2048]{1,0:T(8,128)(2,1)} reshape(bf16[64,1,9,2048]{3,2,0,1:T(8,128)(2,1)} %get-tuple-element.8) | data formatting | bytes 4718592 | tf_op jit(solution)/shard_map/reshape;squeeze | solution.py:127
  471.8 2.4 fusion.23
  474.2 1.3 fusion.13
  (63 shorter events, 7.6 us)
Async XLA Ops:
  0.6 162.7 %copy-start = (bf16[1,2048,704]{1,2,0:T(8,128)(2,1)S(1)}, bf16[1,2048,704]{1,2,0:T(8,128)(2,1)}, u32[]{:S(2)}) copy-start(bf16[1,2048,704]{1,2,0:T(8,128)(2,1)} %param.11) | copy-start | bytes 8650756
  19.9 10.9 %copy-start.9 = (bf16[64,2048]{1,0:T(8,128)(2,1)S(1)}, bf16[64,2048]{1,0:T(8,128)(2,1)}, u32[]{:S(2)}) copy-start(bf16[64,2048]{1,0:T(8,128)(2,1)} %param.8) | copy-start | bytes 786436
  19.9 120.2 %all-to-all-start.2 = ((bf16[128,9,2048]{2,1,0:T(8,128)(2,1)}), bf16[128,9,2048]{2,1,0:T(8,128)(2,1)}, u32[]{:S(2)}, u32[]{:S(2)}) async-start(bf16[128,9,2048]{2,1,0:T(8,128)(2,1)} %bitcast.69), calls=%async_computation.2 | async-start | bytes 16777216 | tf_op jit(solution)/shard_map/all_to_all | solution.py:145
  147.0 117.2 %all-to-all-start.1 = ((bf16[128,9,2048]{2,1,0:T(8,128)(2,1)}), bf16[128,9,2048]{2,1,0:T(8,128)(2,1)}, u32[]{:S(2)}, u32[]{:S(2)}) async-start(bf16[128,9,2048]{2,1,0:T(8,128)(2,1)} %bitcast.68), calls=%async_computation.1 | async-start | bytes 16777216 | tf_op jit(solution)/shard_map/all_to_all | solution.py:146
  163.3 8.2 %copy-start.3 = (bf16[1152,2048]{1,0:T(8,128)(2,1)S(1)}, bf16[1152,2048]{1,0:T(8,128)(2,1)}, u32[]{:S(2)}) copy-start(bf16[1152,2048]{1,0:T(8,128)(2,1)} %reshape_squeeze_reshape.8) | copy-start | bytes 14155780
  163.3 8.2 %copy-start.11 = (bf16[1,2048,704]{1,2,0:T(8,128)(2,1)S(1)}, bf16[1,2048,704]{1,2,0:T(8,128)(2,1)}, u32[]{:S(2)}) copy-start(bf16[1,2048,704]{1,2,0:T(8,128)(2,1)} %param.12) | copy-start | bytes 8650756
  272.7 20.6 %copy-start.10 = (bf16[64,6]{0,1:T(8,128)(2,1)S(1)}, bf16[64,6]{0,1:T(8,128)(2,1)}, u32[]{:S(2)}) copy-start(bf16[64,6]{0,1:T(8,128)(2,1)} %param.9) | copy-start | bytes 2308
  284.3 18.0 %all-to-all-start.4 = ((bf16[128,1,9]{2,1,0:T(2,128)(2,1)}), bf16[128,1,9]{2,1,0:T(2,128)(2,1)S(1)}, u32[]{:S(2)}, u32[]{:S(2)}) async-start(bf16[128,1,9]{2,1,0:T(2,128)(2,1)} %convert_element_type.103), calls=%async_computation.4 | async-start | bytes 131072 | tf_op jit(solution)/shard_map/all_to_all | solution.py:154
  322.8 4.0 copy-start.6
  322.8 4.0 copy-start.8
  322.9 4.0 copy-start.12
  340.4 14.7 %slice-start = ((s8[4718592]{0:T(1024)(128)(4,1)}), s8[524288]{0:T(1024)(128)(4,1)S(1)}, s32[]{:S(2)}) async-start(s8[4718592]{0:T(1024)(128)(4,1)} %bitcast.70), calls=%async_computation.5 | async-start | bytes 1048576
  340.4 115.6 %all-to-all-start.3 = ((bf16[128,9,2048]{2,1,0:T(8,128)(2,1)}), bf16[128,9,2048]{2,1,0:T(8,128)(2,1)}, u32[]{:S(2)}, u32[]{:S(2)}) async-start(bf16[128,9,2048]{2,1,0:T(8,128)(2,1)} %reshape_stack_reshape.4), calls=%async_computation.3 | async-start | bytes 16777216 | tf_op jit(solution)/shard_map/all_to_all | solution.py:153
  346.7 8.5 %slice-start.1 = ((s8[4718592]{0:T(1024)(128)(4,1)}), s8[4194304]{0:T(1024)(128)(4,1)S(1)}, s32[]{:S(2)}) async-start(s8[4718592]{0:T(1024)(128)(4,1)} %bitcast.70), calls=%async_computation.6 | async-start | bytes 8388608
  346.7 8.5 %copy-start.7 = (bf16[1152,704]{0,1:T(8,128)(2,1)S(1)}, bf16[1152,704]{0,1:T(8,128)(2,1)}, u32[]{:S(2)}) copy-start(bf16[1152,704]{0,1:T(8,128)(2,1)} %copy-done.6) | copy-start | bytes 4866052
  346.7 13.7 %slice-start.2 = ((s8[4718592]{0:T(1024)(128)(4,1)}), s8[4194304]{0:T(1024)(128)(4,1)S(1)}, s32[]{:S(2)}) async-start(s8[4718592]{0:T(1024)(128)(4,1)} %bitcast.72), calls=%async_computation.7 | async-start | bytes 8388608
  355.2 5.2 %slice-start.3 = ((s8[4718592]{0:T(1024)(128)(4,1)}), s8[524288]{0:T(1024)(128)(4,1)S(1)}, s32[]{:S(2)}) async-start(s8[4718592]{0:T(1024)(128)(4,1)} %bitcast.72), calls=%async_computation.8 | async-start | bytes 1048576
  355.2 5.2 %copy-start.4 = (f32[1152,704]{0,1:T(8,128)S(1)}, f32[1152,704]{0,1:T(8,128)}, u32[]{:S(2)}) copy-start(f32[1152,704]{0,1:T(8,128)} %fusion.6) | copy-start | bytes 9732100
  355.2 5.2 %copy-start.5 = (f32[1152,704]{0,1:T(8,128)S(1)}, f32[1152,704]{0,1:T(8,128)}, u32[]{:S(2)}) copy-start(f32[1152,704]{0,1:T(8,128)} %fusion.9) | copy-start | bytes 9732100
  466.9 8.6 %copy-start.1 = (bf16[1,2048,704]{1,2,0:T(8,128)(2,1)S(1)}, bf16[1,2048,704]{1,2,0:T(8,128)(2,1)}, u32[]{:S(2)}) copy-start(bf16[1,2048,704]{1,2,0:T(8,128)(2,1)} %param.11) | copy-start | bytes 8650756
  471.8 2.4 copy-start.2
where the time goes:
time: 478 us; the launch traced here: 475 us
  waiting for transfers between devices  289 us (60%)
  local copies, waits for them, and re-layouts  67 us (14%)
  matrix products  62.2 us (13%)
  starting transfers between devices  33.9 us (7%)
  blocking collectives  13.9 us (3%)
  other arithmetic  8.85 us (2%)
    all_to_all x1, waiting for transfers between devices, local(): lax.all_to_all(packed[0], ('node', 'local'), split_axis=0, concat_axis=0,...  102 us
    all_to_all x1, waiting for transfers between devices, local(): lax.all_to_all(term_back, ('node', 'local'), split_axis=0, concat_axis=0,...  90.2 us
    all_to_all x1, waiting for transfers between devices, local(): lax.all_to_all(packed[1], ('node', 'local'), split_axis=0, concat_axis=0,...  87 us
    all_to_all x1, blocking collectives, local(): lax.all_to_all(packed[2], ('node', 'local'), split_axis=0, concat_axis=0,...  13.9 us
    broadcast_in_dim x3, local copies, waits for them, and re-layouts, spread_rows(): return jnp.repeat(shaped, halves, axis=0)  13.6 us
    all_to_all x1, starting transfers between devices, local(): lax.all_to_all(packed[0], ('node', 'local'), split_axis=0, concat_axis=0,...  10.9 us
    dot_general x1, matrix products, unit_pass(): lax.dot_general(rows_dy, down_w, contract_cols, preferred_element_type=jn...  10.8 us
  transfers between devices with their start and end apart: 4, of which 4 were waited for; matrix products, arithmetic and copies ran while one was open for 10% of the time, Pallas kernels for 0%

commit v1 on v0

v1 whole, which is shorter than its diff:
```python
import jax
import jax.numpy as jnp
from jax import lax
from jax.experimental import pallas as pl
from jax.experimental.pallas import tpu as pltpu
from jax.sharding import PartitionSpec as P

LOW = 8
BF = jnp.bfloat16
F32 = jnp.float32
AXES = ("node", "local")
NT = (((1,), (1,)), ((), ()))
TN = (((0,), (0,)), ((), ()))


def dot(a, b, dims=(((1,), (0,)), ((), ()))):
    return lax.dot_general(a, b, dims, preferred_element_type=F32)


def column_tables(ids, first, columns, halves):
    tokens = ids.shape[0]
    col = lax.broadcasted_iota(jnp.int32, (tokens, columns), 1)
    expert = first + col // (halves * LOW)
    row = col % LOW
    hit = jnp.zeros((tokens, columns), F32)
    for k in range(ids.shape[1]):
        hit = hit + jnp.where(ids[:, k : k + 1] == expert, 1.0, 0.0)
    before = lax.broadcasted_iota(jnp.int32, (tokens, tokens), 1) < lax.broadcasted_iota(
        jnp.int32, (tokens, tokens), 0
    )
    rank = dot(jnp.where(before, 1.0, 0.0).astype(BF), hit.astype(BF)).astype(jnp.int32)
    return expert, row, hit, rank


def pack_kernel(halves, ids_ref, gates_ref, x_ref, dy_ref, out_ref):
    columns, width = out_ref.shape[0], x_ref.shape[1]
    ids = ids_ref[...]
    gates = gates_ref[...].astype(F32)
    first = pl.program_id(0) * (columns // (halves * LOW))
    expert, row, hit, rank = column_tables(ids, first, columns, halves)
    gate = jnp.zeros(hit.shape, F32)
    for k in range(ids.shape[1]):
        gate = gate + jnp.where(ids[:, k : k + 1] == expert, gates[:, k : k + 1], 0.0)
    low = jnp.where(rank == row, hit, 0.0)
    x, dy = x_ref[...], dy_ref[...]
    out_ref[:, :width] = dot(low.astype(BF), x, TN).astype(BF)
    out_ref[:, width : 2 * width] = dot((low * gate).astype(BF), dy, TN).astype(BF)
    last = jnp.where(rank == LOW, hit, 0.0)
    piece = 2 * width // LOW
    masks, pieces = [], []
    for i in range(LOW):
        at = i * piece
        source, weight = (x, last) if at < width else (dy, last * gate)
        masks.append(jnp.where(row == i, weight, 0.0).astype(BF))
        pieces.append(source[:, at % width : at % width + piece])
    out_ref[:, 2 * width :] = dot(
        jnp.concatenate(masks, 0), jnp.concatenate(pieces, 0), TN
    ).astype(BF)


def piece_table(sources):
    shape = (sources * LOW, sources * LOW)
    a = lax.broadcasted_iota(jnp.int32, shape, 0)
    b = lax.broadcasted_iota(jnp.int32, shape, 1)
    return jnp.where((a % sources) * LOW + a // sources == b, 1.0, 0.0).astype(BF)


def unit_kernel(
    got_ref, gate_ref, up_ref, down_ref,
    back_ref, dg_ref, du_ref, act_ref, dg9_ref, du9_ref, act9_ref, x9_ref, dy9_ref,
):
    rows, width = got_ref.shape[0], gate_ref.shape[1]
    sources = rows // LOW
    table = piece_table(sources)
    nine = dot(table, got_ref[:, 2 * width :]).astype(BF)
    nine = [nine[i * sources : (i + 1) * sources] for i in range(LOW)]
    x9 = jnp.concatenate(nine[: LOW // 2], 1)
    dy9 = jnp.concatenate(nine[LOW // 2 :], 1)
    x9_ref[...] = x9
    dy9_ref[...] = dy9
    x = jnp.concatenate([got_ref[:, :width], x9], 0)
    dy = jnp.concatenate([got_ref[:, width : 2 * width], dy9], 0)
    gate_w, up_w, down_w = gate_ref[...], up_ref[...], down_ref[...]
    pre_gate = dot(x, gate_w, NT)
    pre_up = dot(x, up_w, NT)
    back = dot(dy, down_w, NT)
    sig = jax.nn.sigmoid(pre_gate)
    silu = pre_gate * sig
    act = silu * pre_up
    part = jnp.sum(act * back, axis=1, keepdims=True)
    d_gate = (back * pre_up * sig * (1.0 + pre_gate * (1.0 - sig))).astype(BF)
    d_up = (back * silu).astype(BF)
    act = act.astype(BF)
    dg_ref[...], dg9_ref[...] = d_gate[:rows], d_gate[rows:]
    du_ref[...], du9_ref[...] = d_up[:rows], d_up[rows:]
    act_ref[...], act9_ref[...] = act[:rows], act[rows:]
    term = (dot(d_gate, gate_w) + dot(d_up, up_w)).astype(BF)
    back_ref[:, :width] = term[:rows]
    piece = width // LOW
    term9 = jnp.concatenate(
        [term[rows:, i * piece : (i + 1) * piece] for i in range(LOW)], 0
    )
    back_ref[:, width : width + piece] = dot(table, term9, TN).astype(BF)
    lane = lax.broadcasted_iota(jnp.int32, (rows, 128), 1)
    lane9 = lax.broadcasted_iota(jnp.int32, (sources, 128), 1)
    part9 = jnp.where(lane9 == 1, part[rows:], 0.0).astype(BF)
    parts = jnp.where(lane == 0, part[:rows], 0.0) + dot(table[:sources], part9, TN)
    back_ref[:, width + piece :] = parts.astype(BF)


def collect_kernel(halves, ids_ref, gates_ref, back_ref, out_ref, gg_ref, sum_ref, part_ref):
    columns, width = back_ref.shape[0], out_ref.shape[1]
    step = pl.program_id(0)
    ids = ids_ref[...]
    top = ids.shape[1]
    first = step * (columns // (halves * LOW))
    expert, row, hit, rank = column_tables(ids, first, columns, halves)
    low = jnp.where(rank == row, hit, 0.0)
    last = jnp.where(rank == LOW, hit, 0.0)

    @pl.when(step == 0)
    def _():
        sum_ref[...] = jnp.zeros_like(sum_ref)
        part_ref[...] = jnp.zeros_like(part_ref)

    piece = width // LOW
    sum_ref[...] += dot(low.astype(BF), back_ref[:, :width])
    pieces = back_ref[:, width : width + piece]
    for i in range(LOW):
        mask = jnp.where(row == i, last, 0.0).astype(BF)
        sum_ref[:, i * piece : (i + 1) * piece] += dot(mask, pieces)
    parts = back_ref[:, width + piece :]
    head = jnp.where(row == 0, last, 0.0)
    lane = lax.broadcasted_iota(jnp.int32, (ids.shape[0], 128), 1)
    for k in range(top):
        mine = ids[:, k : k + 1] == expert
        got = dot(jnp.where(mine, low, 0.0).astype(BF), parts)
        got9 = dot(jnp.where(mine, head, 0.0).astype(BF), parts)
        both = jnp.sum(
            jnp.where(lane == 0, got, 0.0) + jnp.where(lane == 1, got9, 0.0), axis=1, keepdims=True
        )
        part_ref[...] += jnp.where(lane == k, both, 0.0)

    @pl.when(step == pl.num_programs(0) - 1)
    def _():
        out_ref[...] = sum_ref[...].astype(BF)
        gg_ref[...] = part_ref[:, :top] / gates_ref[...].astype(F32)


def whole(shape):
    return pl.BlockSpec(shape, lambda b: (0,) * len(shape))


def split(shape):
    return pl.BlockSpec(shape, lambda b: (b,) + (0,) * (len(shape) - 1))


def limits(mib):
    return pltpu.CompilerParams(
        dimension_semantics=("arbitrary",), vmem_limit_bytes=mib * 2**20
    )


def local(tokens, cotangent, gate_weights, expert_ids, gate_proj, up_proj, down_proj):
    devices = lax.axis_size("node") * lax.axis_size("local")
    count, width = tokens.shape
    hidden = down_proj.shape[1]
    halves = 2
    experts = devices // halves
    slots = devices * LOW
    top = expert_ids.shape[1]

    blocks = 4
    message = 2 * width + 2 * width // LOW
    sent = pl.pallas_call(
        lambda *refs: pack_kernel(halves, *refs),
        grid=(blocks,),
        in_specs=[
            whole((count, top)), whole((count, top)), whole((count, width)), whole((count, width)),
        ],
        out_specs=split((slots // blocks, message)),
        out_shape=jax.ShapeDtypeStruct((slots, message), BF),
        compiler_params=limits(48),
        name="pack_rows",
    )(expert_ids, gate_weights, tokens, cotangent)

    got = lax.all_to_all(
        sent.reshape(devices, LOW, message), AXES, split_axis=0, concat_axis=0, tiled=True
    ).reshape(slots, message)

    gate_t = jnp.swapaxes(gate_proj[0], 0, 1)
    up_t = jnp.swapaxes(up_proj[0], 0, 1)
    down = down_proj[0]
    blocks = 4
    rows, rows9 = slots // blocks, devices // blocks
    reply = width + width // LOW + 128
    weight = pl.BlockSpec((hidden, width), lambda b: (0, 0), pipeline_mode=pl.Buffered(1))
    term, d_gate, d_up, act, d_gate9, d_up9, act9, x9, dy9 = pl.pallas_call(
        unit_kernel,
        grid=(blocks,),
        in_specs=[split((rows, message)), weight, weight, weight],
        out_specs=[split((rows, reply))]
        + [split((rows, hidden))] * 3
        + [split((rows9, hidden))] * 3
        + [split((rows9, width))] * 2,
        out_shape=[jax.ShapeDtypeStruct((slots, reply), BF)]
        + [jax.ShapeDtypeStruct((slots, hidden), BF)] * 3
        + [jax.ShapeDtypeStruct((devices, hidden), BF)] * 3
        + [jax.ShapeDtypeStruct((devices, width), BF)] * 2,
        compiler_params=limits(60),
        name="unit_terms",
    )(got, gate_t, up_t, down)

    returned = lax.all_to_all(
        term.reshape(devices, LOW, reply), AXES, split_axis=0, concat_axis=0, tiled=True
    ).reshape(slots, reply)

    x8, dy8 = got[:, :width], got[:, width : 2 * width]
    grad_gate = (dot(x8, d_gate, TN) + dot(x9, d_gate9, TN)).astype(BF)
    grad_up = (dot(x8, d_up, TN) + dot(x9, d_up9, TN)).astype(BF)
    grad_down = (dot(act, dy8, TN) + dot(act9, dy9, TN)).astype(BF)

    blocks = 4
    grad_tokens, grad_gates = pl.pallas_call(
        lambda *refs: collect_kernel(halves, *refs),
        grid=(blocks,),
        in_specs=[whole((count, top)), whole((count, top)), split((slots // blocks, reply))],
        out_specs=[whole((count, width)), whole((count, top))],
        out_shape=[
            jax.ShapeDtypeStruct((count, width), BF),
            jax.ShapeDtypeStruct((count, top), F32),
        ],
        scratch_shapes=[pltpu.VMEM((count, width), F32), pltpu.VMEM((count, 128), F32)],
        compiler_params=limits(48),
        name="collect_rows",
    )(expert_ids, gate_weights, returned)
    return grad_tokens, grad_gates, grad_gate[None], grad_up[None], grad_down[None]


def solution(mesh):
    row = P(AXES, None)
    unit = P(AXES, None, None)
    return jax.shard_map(
        local,
        mesh=mesh,
        in_specs=(row, row, row, row, unit, unit, unit),
        out_specs=(row, row, unit, unit, unit),
        check_vma=False,
    )
```

time: 478 us -> 238 us (0.50)
  waiting for transfers between devices: 289 us -> 43 us
  blocking collectives: 13.9 us -> 121 us
  local copies, waits for them, and re-layouts: 67 us -> 4.18 us
  matrix products: 62.2 us -> 19.2 us
  Pallas kernels: 0 us -> 42 us
  starting transfers between devices: 33.9 us -> 6.92 us
  other arithmetic: 8.85 us -> 0.01 us
    all_to_all x4 -> x1, waiting for transfers between devices: 289 us -> 43 us  [local(): lax.all_to_all(term.reshape(devices, LOW, reply), AXES, split_axis=0, con...]
    all_to_all x1, blocking collectives: 13.9 us -> 121 us  [local(): lax.all_to_all(sent.reshape(devices, LOW, message), AXES, split_axis=0, c...]
    dot_general x12 -> x6, matrix products: 62.2 us -> 19.2 us  [dot(): return lax.dot_general(a, b, dims, preferred_element_type=F32)]
    pallas_call x0 -> x3, Pallas kernels: none -> 42 us  [the longest x1 29.2 us: local(): pl.pallas_call(unit_kernel, grid=(blocks,), in_specs=[split((rows, messag...]
    another operation x5 -> x0, local copies, waits for them, and re-layouts: 34.6 us -> none  [the longest x2 9.56 us: collect(): shaped[:, half].reshape(-1, width)]
    all_to_all x4 -> x1, starting transfers between devices: 33.9 us -> 6.92 us  [local(): lax.all_to_all(term.reshape(devices, LOW, reply), AXES, split_axis=0, con...]
    broadcast_in_dim x4 -> x0, local copies, waits for them, and re-layouts: 13.8 us -> none  [the longest x3 13.6 us: spread_rows(): return jnp.repeat(shaped, halves, axis=0)]
    reshape x4 -> x0, local copies, waits for them, and re-layouts: 9.4 us -> none  [the longest x2 9.19 us: spread_rows(): shaped = rows.reshape((expert_count, slot_depth) + rows.shape[1:])]
  transfers between devices with their start and end apart: 4 -> 1, of which waited for: 4 -> 1; matrix products, arithmetic and copies ran while one was open for 10% -> 8% of each run, Pallas kernels for 0% -> 0%
where the time goes in v1:
time: 238 us
  blocking collectives  121 us (51%)
  waiting for transfers between devices  43 us (18%)
  Pallas kernels  42 us (18%)
  matrix products  19.2 us (8%)
  starting transfers between devices  6.92 us (3%)
  local copies, waits for them, and re-layouts  4.18 us (2%)
    all_to_all x1, blocking collectives, local(): lax.all_to_all(sent.reshape(devices, LOW, message), AXES, split_axis=0, c...  121 us
    all_to_all x1, waiting for transfers between devices, local(): lax.all_to_all(term.reshape(devices, LOW, reply), AXES, split_axis=0, con...  43 us
    pallas_call x1, Pallas kernels, local(): pl.pallas_call(unit_kernel, grid=(blocks,), in_specs=[split((rows, messag...  29.2 us
    dot_general x6, matrix products, dot(): return lax.dot_general(a, b, dims, preferred_element_type=F32)  19.2 us
    all_to_all x1, starting transfers between devices, local(): lax.all_to_all(term.reshape(devices, LOW, reply), AXES, split_axis=0, con...  6.92 us
    pallas_call x1, Pallas kernels, local(): pl.pallas_call(lambda *refs: pack_kernel(halves, *refs), grid=(blocks,),...  6.41 us
    pallas_call x1, Pallas kernels, local(): pl.pallas_call(lambda *refs: collect_kernel(halves, *refs), grid=(blocks,...  6.35 us
  transfers between devices with their start and end apart: 1, of which 1 were waited for; matrix products, arithmetic and copies ran while one was open for 8% of the time, Pallas kernels for 0%

profile of v1, /device:TPU:8, one launch (start us, length us, event | category | flops | bytes accessed | tf_op | source)
XLA Modules:
  0.0 237.6 jit_solution(16683829223367260473)
XLA Ops:
  0.6 0.8 copy.14.refs_0_
  1.4 0.8 copy.15.refs_1_
  2.2 0.9 copy-done
  3.1 0.9 copy-done.1
  4.1 6.4 %pack_rows.1 = bf16[1024,4608]{1,0:T(8,128)(2,1)} custom-call(s32[64,6]{1,0:T(8,128)S(1)} %copy.14.refs_0_, bf16[64,6]{1,0:T(8,128)(2,1)S(1)} %copy.15.refs_1_, bf16[64,2048]{1,0:T(8,128)(2,1)S(1)} %copy-done, bf16[64,2048]{1,0:T(8,128)(2,1)S(1)} %copy-done.1), custom_call_target="tpu_custom_call" | custom-call | tf_op jit(solution)/shard_map/pack_rows/pallas_call | solution.py:175
  10.5 121.5 %all_to_all.10 = bf16[128,8,4608]{2,1,0:T(8,128)(2,1)} all-to-all(bf16[128,8,4608]{2,1,0:T(8,128)(2,1)} %bitcast.32), channel_id=1, replica_groups=mesh['node'=8,'local'=16] {'node','local'}, dimensions={0} | all-to-all | bytes 18874368 | tf_op jit(solution)/shard_map/all_to_all | solution.py:187
  132.0 29.2 %unit_terms.1 = (bf16[1024,2432]{1,0:T(8,128)(2,1)}, bf16[1024,704]{1,0:T(8,128)(2,1)}, bf16[1024,704]{1,0:T(8,128)(2,1)}, bf16[1024,704]{1,0:T(8,128)(2,1)}, bf...) custom-call(bf16[1024,4608]{1,0:T(8,128)(2,1)} %bitcast.26, ...), custom_call_target="tpu_custom_call" | custom-call | tf_op jit(solution)/shard_map/unit_terms/pallas_call | solution.py:198
  161.2 0.0 copy-start.9
  161.2 0.0 slice-start
  161.2 6.9 %all-to-all-start.1 = ((bf16[128,8,2432]{2,1,0:T(8,128)(2,1)}), bf16[128,8,2432]{2,1,0:T(8,128)(2,1)}, u32[]{:S(2)}, u32[]{:S(2)}) async-start(bf16[128,8,2432]{2,1,0:T(8,128)(2,1)} %bitcast.33), calls=%async_computation.1 | async-start | bytes 9961472 | tf_op jit(solution)/shard_map/all_to_all | solution.py:214
  168.2 0.0 copy-done.9
  168.2 0.0 copy-start.2
  168.2 0.0 copy-start.7
  168.2 0.0 slice-start.1
  168.2 0.0 slice-start.2
  168.2 5.2 %fusion.4 = f32[2048,704]{0,1:T(8,128)S(1)} fusion(bf16[1024,704]{1,0:T(8,128)(2,1)S(1)} %copy-done.9, bf16[1024,4608]{1,0:T(8,128)(2,1)} %bitcast.27), kind=kOutput, calls=%fused_computation.7 | convolution fusion | flops 2952790016 | bytes 11403264 | tf_op jit(solution)/shard_map/dot_general | solution.py:17
  173.4 0.0 copy-done.2
  173.4 0.0 copy-done.7
  173.4 0.0 copy-start.8
  173.4 2.5 %fusion.6 = bf16[1,2048,704]{1,2,0:T(8,128)(2,1)} fusion(f32[2048,704]{0,1:T(8,128)S(1)} %fusion.4, bf16[128,2048]{1,0:T(8,128)(2,1)S(1)} %copy-done.2, bf16[128,704]{1,0:T(8,128)(2,1)S(1)} %copy-done.7), kind=kOutput, calls=%fused_computation.9 | convolution fusion | flops 371982336 | bytes 9355264 | tf_op jit(solution)/shard_map/dot_general | solution.py:17
  176.0 0.0 slice-done
  176.0 0.0 slice-done.1
  176.0 0.0 slice-done.2
  176.0 0.0 copy-done.8
  176.0 0.0 copy-start.6
  176.0 3.2 %fusion.2 = f32[2048,704]{0,1:T(8,128)S(1)} fusion(bf16[1024,704]{1,0:T(8,128)(2,1)S(1)} %copy-done.8, bf16[1024,4608]{1,0:T(8,128)(2,1)S(1)} %bitcast.30), kind=kOutput, calls=%fused_computation.5 | convolution fusion | flops 2952790016 | bytes 11534336 | tf_op jit(solution)/shard_map/dot_general | solution.py:17
  179.2 2.5 %fusion.7 = bf16[1,2048,704]{1,2,0:T(8,128)(2,1)} fusion(f32[2048,704]{0,1:T(8,128)S(1)} %fusion.2, bf16[128,2048]{1,0:T(8,128)(2,1)S(1)} %copy-done.2, bf16[128,704]{1,0:T(8,128)(2,1)S(1)} %copy-done.6), kind=kOutput, calls=%fused_computation.10 | convolution fusion | flops 371982336 | bytes 9355264 | tf_op jit(solution)/shard_map/dot_general | solution.py:17
  181.8 3.2 %fusion = f32[704,2048]{1,0:T(8,128)S(1)} fusion(bf16[1024,704]{1,0:T(8,128)(2,1)S(1)} %copy-done.3, bf16[1024,4608]{1,0:T(8,128)(2,1)S(1)} %bitcast.31), kind=kOutput, calls=%fused_computation.3 | convolution fusion | flops 2952790016 | bytes 11534336 | tf_op jit(solution)/shard_map/dot_general | solution.py:17
  185.0 2.5 %fusion.8 = bf16[1,704,2048]{2,1,0:T(8,128)(2,1)} fusion(f32[704,2048]{1,0:T(8,128)S(1)} %fusion, bf16[128,704]{1,0:T(8,128)(2,1)S(1)} %copy-done.5, bf16[128,2048]{1,0:T(8,128)(2,1)S(1)} %copy-done.4), kind=kOutput, calls=%fused_computation.11 | convolution fusion | flops 371982336 | bytes 9355264 | tf_op jit(solution)/shard_map/dot_general | solution.py:17
  187.5 43.0 %all-to-all-done.1 = bf16[128,8,2432]{2,1,0:T(8,128)(2,1)} async-done(((bf16[128,8,2432]{2,1,0:T(8,128)(2,1)}), bf16[128,8,2432]{2,1,0:T(8,128)(2,1)}, u32[]{:S(2)}, u32[]{:S(2)}) %all-to-all-start.1) | async-done | bytes 4980768 | tf_op jit(solution)/shard_map/all_to_all | solution.py:214
  230.5 6.4 %collect_rows.1 = (bf16[64,2048]{1,0:T(8,128)(2,1)}, f32[64,6]{1,0:T(8,128)S(1)}) custom-call(s32[64,6]{1,0:T(8,128)S(1)} %copy.14.refs_0_, bf16[64,6]{1,0:T(8,128)(2,1)S(1)} %copy.15.refs_1_, bf16[1024,2432]{1,0:T(8,128)(2,1)} %bitcast.8.refs_2_), custom_call_target="tpu_custom_call" | custom-call | tf_op jit(solution)/shard_map/collect_rows/pallas_call | solution.py:224
  236.9 0.7 copy.16
  (10 shorter events, 0.0 us)
Async XLA Ops:
  2.2 1.0 copy-start
  3.1 0.9 copy-start.1
  161.2 7.0 %copy-start.9 = (bf16[1024,704]{1,0:T(8,128)(2,1)S(1)}, bf16[1024,704]{1,0:T(8,128)(2,1)}, u32[]{:S(2)}) copy-start(bf16[1024,704]{1,0:T(8,128)(2,1)} %get-tuple-element.19) | copy-start | bytes 4325380
  161.2 14.8 %slice-start = ((s8[9437184]{0:T(1024)(128)(4,1)}), s8[1048576]{0:T(1024)(128)(4,1)S(1)}, s32[]{:S(2)}) async-start(s8[9437184]{0:T(1024)(128)(4,1)} %bitcast.28), calls=%async_computation.2 | async-start | bytes 2097152
  161.2 69.3 %all-to-all-start.1 = ((bf16[128,8,2432]{2,1,0:T(8,128)(2,1)}), bf16[128,8,2432]{2,1,0:T(8,128)(2,1)}, u32[]{:S(2)}, u32[]{:S(2)}) async-start(bf16[128,8,2432]{2,1,0:T(8,128)(2,1)} %bitcast.33), calls=%async_computation.1 | async-start | bytes 9961472 | tf_op jit(solution)/shard_map/all_to_all | solution.py:214
  168.2 5.2 %copy-start.2 = (bf16[128,2048]{1,0:T(8,128)(2,1)S(1)}, bf16[128,2048]{1,0:T(8,128)(2,1)}, u32[]{:S(2)}) copy-start(bf16[128,2048]{1,0:T(8,128)(2,1)} %get-tuple-element.20) | copy-start | bytes 1572868
  168.2 5.2 %copy-start.7 = (bf16[128,704]{1,0:T(8,128)(2,1)S(1)}, bf16[128,704]{1,0:T(8,128)(2,1)}, u32[]{:S(2)}) copy-start(bf16[128,704]{1,0:T(8,128)(2,1)} %get-tuple-element.21) | copy-start | bytes 540676
  168.2 7.8 %slice-start.1 = ((s8[9437184]{0:T(1024)(128)(4,1)}), s8[4194304]{0:T(1024)(128)(4,1)S(1)}, s32[]{:S(2)}) async-start(s8[9437184]{0:T(1024)(128)(4,1)} %bitcast.28), calls=%async_computation.3 | async-start | bytes 8388608
  168.2 7.8 %slice-start.2 = ((s8[9437184]{0:T(1024)(128)(4,1)}), s8[4194304]{0:T(1024)(128)(4,1)S(1)}, s32[]{:S(2)}) async-start(s8[9437184]{0:T(1024)(128)(4,1)} %bitcast.28), calls=%async_computation.4 | async-start | bytes 8388608
  173.4 2.6 %copy-start.8 = (bf16[1024,704]{1,0:T(8,128)(2,1)S(1)}, bf16[1024,704]{1,0:T(8,128)(2,1)}, u32[]{:S(2)}) copy-start(bf16[1024,704]{1,0:T(8,128)(2,1)} %get-tuple-element.22) | copy-start | bytes 4325380
  176.0 3.2 %copy-start.6 = (bf16[128,704]{1,0:T(8,128)(2,1)S(1)}, bf16[128,704]{1,0:T(8,128)(2,1)}, u32[]{:S(2)}) copy-start(bf16[128,704]{1,0:T(8,128)(2,1)} %get-tuple-element.23) | copy-start | bytes 540676
  179.2 2.5 %copy-start.3 = (bf16[1024,704]{1,0:T(8,128)(2,1)S(1)}, bf16[1024,704]{1,0:T(8,128)(2,1)}, u32[]{:S(2)}) copy-start(bf16[1024,704]{1,0:T(8,128)(2,1)} %get-tuple-element.24) | copy-start | bytes 4325380
  181.8 3.2 %copy-start.4 = (bf16[128,2048]{1,0:T(8,128)(2,1)S(1)}, bf16[128,2048]{1,0:T(8,128)(2,1)}, u32[]{:S(2)}) copy-start(bf16[128,2048]{1,0:T(8,128)(2,1)} %get-tuple-element.26) | copy-start | bytes 1572868
  181.8 3.2 %copy-start.5 = (bf16[128,704]{1,0:T(8,128)(2,1)S(1)}, bf16[128,704]{1,0:T(8,128)(2,1)}, u32[]{:S(2)}) copy-start(bf16[128,704]{1,0:T(8,128)(2,1)} %get-tuple-element.25) | copy-start | bytes 540676

commit v2 on v1

v2 whole, which is shorter than its diff:
```python
import jax
import jax.numpy as jnp
from jax import lax
from jax.experimental import pallas as pl
from jax.experimental.pallas import tpu as pltpu
from jax.sharding import PartitionSpec as P

LOW = 8
BF = jnp.bfloat16
F32 = jnp.float32
AXES = ("node", "local")
NT = (((1,), (1,)), ((), ()))
TN = (((0,), (0,)), ((), ()))


def dot(a, b, dims=(((1,), (0,)), ((), ()))):
    return lax.dot_general(a, b, dims, preferred_element_type=F32)


def row_tables(ids, first, rows, halves):
    tokens = ids.shape[1]
    slot = lax.broadcasted_iota(jnp.int32, (rows, tokens), 0)
    expert = first + slot // (halves * LOW)
    row = slot % LOW
    hit = jnp.zeros((rows, tokens), F32)
    for k in range(ids.shape[0]):
        hit = hit + jnp.where(ids[k : k + 1, :] == expert, 1.0, 0.0)
    before = lax.broadcasted_iota(jnp.int32, (tokens, tokens), 0) < lax.broadcasted_iota(
        jnp.int32, (tokens, tokens), 1
    )
    rank = dot(hit.astype(BF), jnp.where(before, 1.0, 0.0).astype(BF)).astype(jnp.int32)
    return expert, row, hit, rank


def pack_kernel(halves, ids_ref, gates_ref, x_ref, dy_ref, out_ref):
    rows, width = out_ref.shape[0], x_ref.shape[1]
    ids = ids_ref[...]
    gates = gates_ref[...].astype(F32)
    first = pl.program_id(0) * (rows // (halves * LOW))
    expert, row, hit, rank = row_tables(ids, first, rows, halves)
    gate = jnp.zeros(hit.shape, F32)
    for k in range(ids.shape[0]):
        gate = gate + jnp.where(ids[k : k + 1, :] == expert, gates[k : k + 1, :], 0.0)
    low = jnp.where(rank == row, hit, 0.0)
    x, dy = x_ref[...], dy_ref[...]
    out_ref[:, :width] = dot(low.astype(BF), x).astype(BF)
    out_ref[:, width : 2 * width] = dot((low * gate).astype(BF), dy).astype(BF)
    last = jnp.where(rank == LOW, hit, 0.0)
    piece = 2 * width // LOW
    masks, pieces = [], []
    for i in range(LOW):
        at = i * piece
        source, weight = (x, last) if at < width else (dy, last * gate)
        masks.append(jnp.where(row == i, weight, 0.0).astype(BF))
        pieces.append(source[:, at % width : at % width + piece])
    out_ref[:, 2 * width :] = dot(
        jnp.concatenate(masks, 1), jnp.concatenate(pieces, 0)
    ).astype(BF)


def piece_table(sources):
    shape = (sources * LOW, sources * LOW)
    a = lax.broadcasted_iota(jnp.int32, shape, 0)
    b = lax.broadcasted_iota(jnp.int32, shape, 1)
    return jnp.where((a % sources) * LOW + a // sources == b, 1.0, 0.0).astype(BF)


def nine_rows(got9_ref, rows9):
    block = 32
    table = piece_table(block)
    x9, dy9 = [], []
    for first in range(0, rows9, block):
        pieces = dot(table, got9_ref[first * LOW : (first + block) * LOW, :]).astype(BF)
        pieces = [pieces[i * block : (i + 1) * block] for i in range(LOW)]
        x9.append(jnp.concatenate(pieces[: LOW // 2], 1))
        dy9.append(jnp.concatenate(pieces[LOW // 2 :], 1))
    return jnp.concatenate(x9, 0), jnp.concatenate(dy9, 0)


def unit_rows(x, dy, gate_ref, up_ref, down_ref, dg_ref, du_ref, act_ref):
    pre_gate = dot(gate_ref[...], x, NT)
    pre_up = dot(up_ref[...], x, NT)
    back = dot(down_ref[...], dy, NT)
    sig = jax.nn.sigmoid(pre_gate)
    silu = pre_gate * sig
    act = silu * pre_up
    part = jnp.sum(act * back, axis=0, keepdims=True)
    d_gate = (back * pre_up * sig * (1.0 + pre_gate * (1.0 - sig))).astype(BF)
    d_up = (back * silu).astype(BF)
    dg_ref[...], du_ref[...], act_ref[...] = d_gate, d_up, act.astype(BF)
    term = dot(d_gate, gate_ref[...], TN) + dot(d_up, up_ref[...], TN)
    return term.astype(BF), jnp.transpose(jnp.broadcast_to(part, (128, part.shape[1])))


def unit_kernel(
    got_ref, got9_ref, gate_ref, up_ref, down_ref,
    back_ref, dg_ref, du_ref, act_ref, dg9_ref, du9_ref, act9_ref, x9_ref, dy9_ref, tail_ref,
):
    rows, width = got_ref.shape[0], gate_ref.shape[1]
    rows9 = x9_ref.shape[0]
    piece = width // LOW
    block = 32
    step = pl.program_id(0)

    @pl.when(step == 0)
    def _():
        x9, dy9 = nine_rows(got9_ref, rows9)
        x9_ref[...], dy9_ref[...] = x9, dy9
        term, part = unit_rows(x9, dy9, gate_ref, up_ref, down_ref, dg9_ref, du9_ref, act9_ref)
        table = piece_table(block)
        lane = lax.broadcasted_iota(jnp.int32, (block, 128), 1)
        for first in range(0, rows9, block):
            at = slice(first, first + block)
            to = slice(first * LOW, (first + block) * LOW)
            pieces = [term[at, i * piece : (i + 1) * piece] for i in range(LOW)]
            tail_ref[to, :piece] = dot(table, jnp.concatenate(pieces, 0), TN).astype(BF)
            part9 = jnp.where(lane == 1, part[at], 0.0).astype(BF)
            tail_ref[to, piece:] = dot(table[:block], part9, TN).astype(BF)

    term, part = unit_rows(
        got_ref[:, :width], got_ref[:, width : 2 * width],
        gate_ref, up_ref, down_ref, dg_ref, du_ref, act_ref,
    )
    here = pl.ds(pl.multiple_of(step * rows, rows), rows)
    back_ref[:, :width] = term
    back_ref[:, width : width + piece] = tail_ref[here, :piece]
    lane = lax.broadcasted_iota(jnp.int32, (rows, 128), 1)
    back_ref[:, width + piece :] = jnp.where(
        lane == 0, part, tail_ref[here, piece:].astype(F32)
    ).astype(BF)


def collect_kernel(halves, ids_ref, gates_ref, back_ref, out_ref, gg_ref, sum_ref, part_ref):
    rows, width = back_ref.shape[0], out_ref.shape[1]
    step = pl.program_id(0)
    ids = ids_ref[...]
    top = ids.shape[0]
    first = step * (rows // (halves * LOW))
    expert, row, hit, rank = row_tables(ids, first, rows, halves)
    low = jnp.where(rank == row, hit, 0.0)
    last = jnp.where(rank == LOW, hit, 0.0)

    @pl.when(step == 0)
    def _():
        sum_ref[...] = jnp.zeros_like(sum_ref)
        part_ref[...] = jnp.zeros_like(part_ref)

    piece = width // LOW
    pieces = back_ref[:, width : width + piece]
    total = dot(low.astype(BF), back_ref[:, :width], TN)
    for i in range(LOW):
        mask = jnp.where(row == i, last, 0.0).astype(BF)
        at = slice(i * piece, (i + 1) * piece)
        sum_ref[:, at] += total[:, at] + dot(mask, pieces, TN)
    parts = back_ref[:, width + piece :].astype(F32)
    mine = low * parts[:, 0:1] + jnp.where(row == 0, last, 0.0) * parts[:, 1:2]
    for k in range(top):
        part_ref[k : k + 1, :] += jnp.sum(
            jnp.where(ids[k : k + 1, :] == expert, mine, 0.0), axis=0, keepdims=True
        )

    @pl.when(step == pl.num_programs(0) - 1)
    def _():
        out_ref[...] = sum_ref[...].astype(BF)
        gg_ref[...] = part_ref[:top, :] / gates_ref[...].astype(F32)


def whole(shape):
    return pl.BlockSpec(shape, lambda b: (0,) * len(shape))


def split(shape):
    return pl.BlockSpec(shape, lambda b: (b,) + (0,) * (len(shape) - 1))


def limits(mib):
    return pltpu.CompilerParams(
        dimension_semantics=("arbitrary",), vmem_limit_bytes=mib * 2**20
    )


def local(tokens, cotangent, gate_weights, expert_ids, gate_proj, up_proj, down_proj):
    devices = lax.axis_size("node") * lax.axis_size("local")
    count, width = tokens.shape
    hidden = down_proj.shape[1]
    halves = 2
    experts = devices // halves
    slots = devices * LOW
    top = expert_ids.shape[1]
    ids_t, gates_t = jnp.swapaxes(expert_ids, 0, 1), jnp.swapaxes(gate_weights, 0, 1)

    blocks = 4
    message = 2 * width + 2 * width // LOW
    sent = pl.pallas_call(
        lambda *refs: pack_kernel(halves, *refs),
        grid=(blocks,),
        in_specs=[
            whole((top, count)), whole((top, count)), whole((count, width)), whole((count, width)),
        ],
        out_specs=split((slots // blocks, message)),
        out_shape=jax.ShapeDtypeStruct((slots, message), BF),
        compiler_params=limits(48),
        name="pack_rows",
    )(ids_t, gates_t, tokens, cotangent)

    got = lax.all_to_all(
        sent.reshape(devices, LOW, message), AXES, split_axis=0, concat_axis=0, tiled=True
    ).reshape(slots, message)

    gate_t = jnp.swapaxes(gate_proj[0], 0, 1)
    up_t = jnp.swapaxes(up_proj[0], 0, 1)
    down = down_proj[0]
    blocks = 2
    rows = slots // blocks
    piece = width // LOW
    reply = width + piece + 128
    gate_t, up_t, down = (
        pltpu.with_memory_space_constraint(w, pltpu.VMEM) for w in (gate_t, up_t, down)
    )
    weight = pl.BlockSpec(memory_space=pltpu.VMEM)
    units = pl.BlockSpec((hidden, rows), lambda b: (0, b))
    term, d_gate, d_up, act, d_gate9, d_up9, act9, x9, dy9 = pl.pallas_call(
        unit_kernel,
        grid=(blocks,),
        in_specs=[
            split((rows, message)),
            pl.BlockSpec((slots, 2 * piece), lambda b: (0, LOW)),
            weight, weight, weight,
        ],
        out_specs=[split((rows, reply))]
        + [units] * 3
        + [whole((hidden, devices))] * 3
        + [whole((devices, width))] * 2,
        out_shape=[jax.ShapeDtypeStruct((slots, reply), BF)]
        + [jax.ShapeDtypeStruct((hidden, slots), BF)] * 3
        + [jax.ShapeDtypeStruct((hidden, devices), BF)] * 3
        + [jax.ShapeDtypeStruct((devices, width), BF)] * 2,
        scratch_shapes=[pltpu.VMEM((slots, piece + 128), BF)],
        compiler_params=limits(48),
        name="unit_terms",
    )(got, got, gate_t, up_t, down)

    returned = lax.all_to_all(
        term.reshape(devices, LOW, reply), AXES, split_axis=0, concat_axis=0, tiled=True
    ).reshape(slots, reply)

    x8, dy8 = got[:, :width], got[:, width : 2 * width]
    grad_gate = (dot(d_gate, x8) + dot(d_gate9, x9)).astype(BF)
    grad_up = (dot(d_up, x8) + dot(d_up9, x9)).astype(BF)
    grad_gate, grad_up = jnp.swapaxes(grad_gate, 0, 1), jnp.swapaxes(grad_up, 0, 1)
    grad_down = (dot(act, dy8) + dot(act9, dy9)).astype(BF)

    blocks = 4
    grad_tokens, grad_gates = pl.pallas_call(
        lambda *refs: collect_kernel(halves, *refs),
        grid=(blocks,),
        in_specs=[whole((top, count)), whole((top, count)), split((slots // blocks, reply))],
        out_specs=[whole((count, width)), whole((top, count))],
        out_shape=[
            jax.ShapeDtypeStruct((count, width), BF),
            jax.ShapeDtypeStruct((top, count), F32),
        ],
        scratch_shapes=[pltpu.VMEM((count, width), F32), pltpu.VMEM((8, count), F32)],
        compiler_params=limits(48),
        name="collect_rows",
    )(ids_t, gates_t, returned)
    grad_gates = jnp.swapaxes(grad_gates, 0, 1)
    return grad_tokens, grad_gates, grad_gate[None], grad_up[None], grad_down[None]


def solution(mesh):
    row = P(AXES, None)
    unit = P(AXES, None, None)
    return jax.shard_map(
        local,
        mesh=mesh,
        in_specs=(row, row, row, row, unit, unit, unit),
        out_specs=(row, row, unit, unit, unit),
        check_vma=False,
    )
```

time: 238 us -> 234 us (0.983)
  Pallas kernels: 42 us -> 38.9 us
where the time goes in v2:
time: 234 us
  blocking collectives  121 us (52%)
  waiting for transfers between devices  43.4 us (19%)
  Pallas kernels  38.9 us (17%)
  matrix products  18.8 us (8%)
  starting transfers between devices  6.93 us (3%)
  local copies, waits for them, and re-layouts  3.34 us (1%)
    all_to_all x1, blocking collectives, local(): lax.all_to_all(sent.reshape(devices, LOW, message), AXES, split_axis=0, c...  121 us
    all_to_all x1, waiting for transfers between devices, local(): lax.all_to_all(term.reshape(devices, LOW, reply), AXES, split_axis=0, con...  43.4 us
    pallas_call x1, Pallas kernels, local(): pl.pallas_call(unit_kernel, grid=(blocks,), in_specs=[split((rows, messag...  27.3 us
    dot_general x6, matrix products, dot(): return lax.dot_general(a, b, dims, preferred_element_type=F32)  18.8 us
    all_to_all x1, starting transfers between devices, local(): lax.all_to_all(term.reshape(devices, LOW, reply), AXES, split_axis=0, con...  6.93 us
    pallas_call x1, Pallas kernels, local(): pl.pallas_call(lambda *refs: pack_kernel(halves, *refs), grid=(blocks,),...  5.83 us
    pallas_call x1, Pallas kernels, local(): pl.pallas_call(lambda *refs: collect_kernel(halves, *refs), grid=(blocks,...  5.77 us
  transfers between devices with their start and end apart: 1, of which 1 were waited for; matrix products, arithmetic and copies ran while one was open for 8% of the time, Pallas kernels for 0%

profile of v2, /device:TPU:8, one launch (start us, length us, event | category | flops | bytes accessed | tf_op | source)
XLA Modules:
  0.0 233.6 jit_solution(8767145256301000573)
XLA Ops:
  0.6 0.0 copy-start.3
  0.6 0.9 copy-done.3
  1.6 0.9 copy-done.4
  2.5 0.7 copy-done.5
  3.2 0.7 copy-done.7
  3.9 5.8 %pack_rows.1 = bf16[1024,4608]{1,0:T(8,128)(2,1)} custom-call(s32[6,64]{1,0:T(8,128)S(1)} %bitcast.32, bf16[6,64]{1,0:T(8,128)(2,1)S(1)} %bitcast.34, bf16[64,2048]{1,0:T(8,128)(2,1)S(1)} %copy-done.3, bf16[64,2048]{1,0:T(8,128)(2,1)S(1)} %copy-done.4), custom_call_target="tpu_custom_call" | custom-call | tf_op jit(solution)/shard_map/pack_rows/pallas_call | solution.py:194
  9.7 121.5 %all_to_all.10 = bf16[128,8,4608]{2,1,0:T(8,128)(2,1)} all-to-all(bf16[128,8,4608]{2,1,0:T(8,128)(2,1)} %bitcast.43), channel_id=1, replica_groups=mesh['node'=8,'local'=16] {'node','local'}, dimensions={0} | all-to-all | bytes 18874368 | tf_op jit(solution)/shard_map/all_to_all | solution.py:206
  131.2 0.0 copy-done
  131.2 0.0 copy-done.1
  131.2 0.0 copy-done.2
  131.2 27.3 %unit_terms.1 = (bf16[1024,2432]{1,0:T(8,128)(2,1)}, bf16[704,1024]{1,0:T(8,128)(2,1)}, bf16[704,1024]{1,0:T(8,128)(2,1)}, bf16[704,1024]{1,0:T(8,128)(2,1)}, bf...) custom-call(bf16[1024,4608]{1,0:T(8,128)(2,1)} %bitcast.36, ...), custom_call_target="tpu_custom_call" | custom-call | tf_op jit(solution)/shard_map/unit_terms/pallas_call | solution.py:222
  158.5 0.0 copy-start.16
  158.5 0.0 slice-start
  158.5 6.9 %all-to-all-start.1 = ((bf16[128,8,2432]{2,1,0:T(8,128)(2,1)}), bf16[128,8,2432]{2,1,0:T(8,128)(2,1)}, u32[]{:S(2)}, u32[]{:S(2)}) async-start(bf16[128,8,2432]{2,1,0:T(8,128)(2,1)} %bitcast.44), calls=%async_computation.1 | async-start | bytes 9961472 | tf_op jit(solution)/shard_map/all_to_all | solution.py:243
  165.5 0.0 copy-start.9
  165.5 0.0 copy-start.13
  165.5 0.0 slice-start.1
  165.5 0.0 slice-start.2
  165.5 5.1 %fusion.2 = f32[2048,704]{0,1:T(8,128)S(1)} fusion(bf16[704,1024]{1,0:T(8,128)(2,1)S(1)} %copy-done.16, bf16[1024,4608]{1,0:T(8,128)(2,1)} %bitcast.38), kind=kOutput, calls=%fused_computation.5 | convolution fusion | flops 2952790016 | bytes 11403264 | tf_op jit(solution)/shard_map/dot_general | solution.py:17
  170.7 0.0 copy-start.15
  170.7 2.5 %fusion.6 = bf16[1,2048,704]{1,2,0:T(8,128)(2,1)} fusion(f32[2048,704]{0,1:T(8,128)S(1)} %fusion.2, bf16[704,128]{1,0:T(8,128)(2,1)S(1)} %copy-done.13, bf16[128,2048]{1,0:T(8,128)(2,1)S(1)} %copy-done.9), kind=kOutput, calls=%fused_computation.9 | convolution fusion | flops 371982336 | bytes 9355264 | tf_op jit(solution)/shard_map/dot_general | solution.py:17
  173.2 0.0 slice-done.1
  173.2 3.1 %fusion.4 = f32[2048,704]{0,1:T(8,128)S(1)} fusion(bf16[704,1024]{1,0:T(8,128)(2,1)S(1)} %copy-done.15, bf16[1024,4608]{1,0:T(8,128)(2,1)S(1)} %bitcast.41), kind=kOutput, calls=%fused_computation.7 | convolution fusion | flops 2952790016 | bytes 11403264 | tf_op jit(solution)/shard_map/dot_general | solution.py:17
  176.3 0.0 copy-done.12
  176.3 0.0 copy-start.14
  176.3 2.5 %fusion.7 = bf16[1,2048,704]{1,2,0:T(8,128)(2,1)} fusion(f32[2048,704]{0,1:T(8,128)S(1)} %fusion.4, bf16[704,128]{1,0:T(8,128)(2,1)S(1)} %copy-done.12, bf16[128,2048]{1,0:T(8,128)(2,1)S(1)} %copy-done.9), kind=kOutput, calls=%fused_computation.10 | convolution fusion | flops 371982336 | bytes 9355264 | tf_op jit(solution)/shard_map/dot_general | solution.py:17
  178.8 3.1 %fusion = f32[704,2048]{1,0:T(8,128)S(1)} fusion(bf16[704,1024]{1,0:T(8,128)(2,1)S(1)} %copy-done.14, bf16[1024,4608]{1,0:T(8,128)(2,1)S(1)} %bitcast.42), kind=kOutput, calls=%fused_computation.3 | convolution fusion | flops 2952790016 | bytes 11403264 | tf_op jit(solution)/shard_map/dot_general | solution.py:17
  182.0 0.0 copy-start.6
  182.0 0.0 copy-start.8
  182.0 2.5 %fusion.8 = bf16[1,704,2048]{2,1,0:T(8,128)(2,1)} fusion(f32[704,2048]{1,0:T(8,128)S(1)} %fusion, bf16[704,128]{1,0:T(8,128)(2,1)S(1)} %copy-done.11, bf16[128,2048]{1,0:T(8,128)(2,1)S(1)} %copy-done.10), kind=kOutput, calls=%fused_computation.11 | convolution fusion | flops 371982336 | bytes 9355264 | tf_op jit(solution)/shard_map/dot_general | solution.py:17
  184.5 43.4 %all-to-all-done.1 = bf16[128,8,2432]{2,1,0:T(8,128)(2,1)} async-done(((bf16[128,8,2432]{2,1,0:T(8,128)(2,1)}), bf16[128,8,2432]{2,1,0:T(8,128)(2,1)}, u32[]{:S(2)}, u32[]{:S(2)}) %all-to-all-start.1) | async-done | bytes 4980768 | tf_op jit(solution)/shard_map/all_to_all | solution.py:243
  227.9 5.8 %collect_rows.1 = (bf16[64,2048]{1,0:T(8,128)(2,1)}, f32[6,64]{1,0:T(8,128)}) custom-call(s32[6,64]{1,0:T(8,128)S(1)} %bitcast.33, bf16[6,64]{1,0:T(8,128)(2,1)S(1)} %bitcast.35, bf16[1024,2432]{1,0:T(8,128)(2,1)} %bitcast.10.refs_2_), custom_call_target="tpu_custom_call" | custom-call | tf_op jit(solution)/shard_map/collect_rows/pallas_call | solution.py:254
  (21 shorter events, 0.0 us)
Async XLA Ops:
  0.6 1.0 copy-start.3
  1.6 0.9 copy-start.4
  2.5 0.7 copy-start.5
  3.2 0.7 copy-start.7
  9.7 121.5 %copy-start = (bf16[1,2048,704]{1,2,0:T(8,128)(2,1)S(1)}, bf16[1,2048,704]{1,2,0:T(8,128)(2,1)}, u32[]{:S(2)}) copy-start(bf16[1,2048,704]{1,2,0:T(8,128)(2,1)} %param.11) | copy-start | bytes 8650756
  9.7 121.5 %copy-start.1 = (bf16[1,2048,704]{1,2,0:T(8,128)(2,1)S(1)}, bf16[1,2048,704]{1,2,0:T(8,128)(2,1)}, u32[]{:S(2)}) copy-start(bf16[1,2048,704]{1,2,0:T(8,128)(2,1)} %param.12) | copy-start | bytes 8650756
  9.7 121.5 %copy-start.2 = (bf16[1,704,2048]{2,1,0:T(8,128)(2,1)S(1)}, bf16[1,704,2048]{2,1,0:T(8,128)(2,1)}, u32[]{:S(2)}) copy-start(bf16[1,704,2048]{2,1,0:T(8,128)(2,1)} %param.13) | copy-start | bytes 8650756
  158.5 7.0 %copy-start.16 = (bf16[704,1024]{1,0:T(8,128)(2,1)S(1)}, bf16[704,1024]{1,0:T(8,128)(2,1)}, u32[]{:S(2)}) copy-start(bf16[704,1024]{1,0:T(8,128)(2,1)} %get-tuple-element.19) | copy-start | bytes 4325380
  158.5 14.6 %slice-start = ((s8[9437184]{0:T(1024)(128)(4,1)}), s8[1048576]{0:T(1024)(128)(4,1)S(1)}, s32[]{:S(2)}) async-start(s8[9437184]{0:T(1024)(128)(4,1)} %bitcast.39), calls=%async_computation.2 | async-start | bytes 2097152
  158.5 69.3 %all-to-all-start.1 = ((bf16[128,8,2432]{2,1,0:T(8,128)(2,1)}), bf16[128,8,2432]{2,1,0:T(8,128)(2,1)}, u32[]{:S(2)}, u32[]{:S(2)}) async-start(bf16[128,8,2432]{2,1,0:T(8,128)(2,1)} %bitcast.44), calls=%async_computation.1 | async-start | bytes 9961472 | tf_op jit(solution)/shard_map/all_to_all | solution.py:243
  165.5 5.1 %copy-start.9 = (bf16[128,2048]{1,0:T(8,128)(2,1)S(1)}, bf16[128,2048]{1,0:T(8,128)(2,1)}, u32[]{:S(2)}) copy-start(bf16[128,2048]{1,0:T(8,128)(2,1)} %get-tuple-element.20) | copy-start | bytes 1572868
  165.5 5.1 %copy-start.13 = (bf16[704,128]{1,0:T(8,128)(2,1)S(1)}, bf16[704,128]{1,0:T(8,128)(2,1)}, u32[]{:S(2)}) copy-start(bf16[704,128]{1,0:T(8,128)(2,1)} %get-tuple-element.21) | copy-start | bytes 540676
  165.5 7.6 %slice-start.1 = ((s8[9437184]{0:T(1024)(128)(4,1)}), s8[4194304]{0:T(1024)(128)(4,1)S(1)}, s32[]{:S(2)}) async-start(s8[9437184]{0:T(1024)(128)(4,1)} %bitcast.39), calls=%async_computation.3 | async-start | bytes 8388608
  165.5 7.6 %slice-start.2 = ((s8[9437184]{0:T(1024)(128)(4,1)}), s8[4194304]{0:T(1024)(128)(4,1)S(1)}, s32[]{:S(2)}) async-start(s8[9437184]{0:T(1024)(128)(4,1)} %bitcast.39), calls=%async_computation.4 | async-start | bytes 8388608
  170.7 2.5 %copy-start.15 = (bf16[704,1024]{1,0:T(8,128)(2,1)S(1)}, bf16[704,1024]{1,0:T(8,128)(2,1)}, u32[]{:S(2)}) copy-start(bf16[704,1024]{1,0:T(8,128)(2,1)} %get-tuple-element.22) | copy-start | bytes 4325380
  173.2 3.2 %copy-start.12 = (bf16[704,128]{1,0:T(8,128)(2,1)S(1)}, bf16[704,128]{1,0:T(8,128)(2,1)}, u32[]{:S(2)}) copy-start(bf16[704,128]{1,0:T(8,128)(2,1)} %get-tuple-element.23) | copy-start | bytes 540676
  176.3 2.5 %copy-start.14 = (bf16[704,1024]{1,0:T(8,128)(2,1)S(1)}, bf16[704,1024]{1,0:T(8,128)(2,1)}, u32[]{:S(2)}) copy-start(bf16[704,1024]{1,0:T(8,128)(2,1)} %get-tuple-element.24) | copy-start | bytes 4325380
  178.8 3.1 %copy-start.10 = (bf16[128,2048]{1,0:T(8,128)(2,1)S(1)}, bf16[128,2048]{1,0:T(8,128)(2,1)}, u32[]{:S(2)}) copy-start(bf16[128,2048]{1,0:T(8,128)(2,1)} %get-tuple-element.26) | copy-start | bytes 1572868
  178.8 3.2 %copy-start.11 = (bf16[704,128]{1,0:T(8,128)(2,1)S(1)}, bf16[704,128]{1,0:T(8,128)(2,1)}, u32[]{:S(2)}) copy-start(bf16[704,128]{1,0:T(8,128)(2,1)} %get-tuple-element.25) | copy-start | bytes 540676
  182.0 45.9 %copy-start.6 = (s32[64,6]{0,1:T(8,128)S(1)}, s32[64,6]{0,1:T(8,128)}, u32[]{:S(2)}) copy-start(s32[64,6]{0,1:T(8,128)} %param.10) | copy-start | bytes 4612
  182.0 45.9 %copy-start.8 = (bf16[64,6]{0,1:T(8,128)(2,1)S(1)}, bf16[64,6]{0,1:T(8,128)(2,1)}, u32[]{:S(2)}) copy-start(bf16[64,6]{0,1:T(8,128)(2,1)} %param.9) | copy-start | bytes 2308

commit v3 on v2

--- a/solution.py
+++ b/solution.py
@@ -65,12 +65,12 @@
     return jnp.where((a % sources) * LOW + a // sources == b, 1.0, 0.0).astype(BF)
 
 
-def nine_rows(got9_ref, rows9):
+def nine_rows(got_ref, at, rows9):
     block = 32
     table = piece_table(block)
     x9, dy9 = [], []
     for first in range(0, rows9, block):
-        pieces = dot(table, got9_ref[first * LOW : (first + block) * LOW, :]).astype(BF)
+        pieces = dot(table, got_ref[first * LOW : (first + block) * LOW, at:]).astype(BF)
         pieces = [pieces[i * block : (i + 1) * block] for i in range(LOW)]
         x9.append(jnp.concatenate(pieces[: LOW // 2], 1))
         dy9.append(jnp.concatenate(pieces[LOW // 2 :], 1))
@@ -93,10 +93,10 @@
 
 
 def unit_kernel(
-    got_ref, got9_ref, gate_ref, up_ref, down_ref,
+    got_ref, gate_ref, up_ref, down_ref,
     back_ref, dg_ref, du_ref, act_ref, dg9_ref, du9_ref, act9_ref, x9_ref, dy9_ref, tail_ref,
 ):
-    rows, width = got_ref.shape[0], gate_ref.shape[1]
+    rows, width = back_ref.shape[0], gate_ref.shape[1]
     rows9 = x9_ref.shape[0]
     piece = width // LOW
     block = 32
@@ -104,7 +104,7 @@
 
     @pl.when(step == 0)
     def _():
-        x9, dy9 = nine_rows(got9_ref, rows9)
+        x9, dy9 = nine_rows(got_ref, 2 * width, rows9)
         x9_ref[...], dy9_ref[...] = x9, dy9
         term, part = unit_rows(x9, dy9, gate_ref, up_ref, down_ref, dg9_ref, du9_ref, act9_ref)
         table = piece_table(block)
@@ -117,11 +117,11 @@
             part9 = jnp.where(lane == 1, part[at], 0.0).astype(BF)
             tail_ref[to, piece:] = dot(table[:block], part9, TN).astype(BF)
 
+    here = pl.ds(pl.multiple_of(step * rows, rows), rows)
     term, part = unit_rows(
-        got_ref[:, :width], got_ref[:, width : 2 * width],
+        got_ref[here, :width], got_ref[here, width : 2 * width],
         gate_ref, up_ref, down_ref, dg_ref, du_ref, act_ref,
     )
-    here = pl.ds(pl.multiple_of(step * rows, rows), rows)
     back_ref[:, :width] = term
     back_ref[:, width : width + piece] = tail_ref[here, :piece]
     lane = lax.broadcasted_iota(jnp.int32, (rows, 128), 1)
@@ -130,39 +130,30 @@
     ).astype(BF)
 
 
-def collect_kernel(halves, ids_ref, gates_ref, back_ref, out_ref, gg_ref, sum_ref, part_ref):
+def collect_kernel(halves, ids_ref, gates_ref, back_ref, out_ref, gg_ref):
     rows, width = back_ref.shape[0], out_ref.shape[1]
-    step = pl.program_id(0)
     ids = ids_ref[...]
-    top = ids.shape[0]
-    first = step * (rows // (halves * LOW))
-    expert, row, hit, rank = row_tables(ids, first, rows, halves)
+    top, count = ids.shape
+    expert, row, hit, rank = row_tables(ids, 0, rows, halves)
     low = jnp.where(rank == row, hit, 0.0)
     last = jnp.where(rank == LOW, hit, 0.0)
-
-    @pl.when(step == 0)
-    def _():
-        sum_ref[...] = jnp.zeros_like(sum_ref)
-        part_ref[...] = jnp.zeros_like(part_ref)
-
     piece = width // LOW
-    pieces = back_ref[:, width : width + piece]
-    total = dot(low.astype(BF), back_ref[:, :width], TN)
+    masks = jnp.concatenate(
+        [jnp.where(row == i, last, 0.0).astype(BF) for i in range(LOW)], 1
+    )
+    pieces = dot(masks, back_ref[:, width : width + piece], TN)
+    low_t = low.astype(BF)
     for i in range(LOW):
-        mask = jnp.where(row == i, last, 0.0).astype(BF)
         at = slice(i * piece, (i + 1) * piece)
-        sum_ref[:, at] += total[:, at] + dot(mask, pieces, TN)
+        total = dot(low_t, back_ref[:, at], TN) + pieces[i * count : (i + 1) * count]
+        out_ref[:, at] = total.astype(BF)
     parts = back_ref[:, width + piece :].astype(F32)
     mine = low * parts[:, 0:1] + jnp.where(row == 0, last, 0.0) * parts[:, 1:2]
     for k in range(top):
-        part_ref[k : k + 1, :] += jnp.sum(
+        part = jnp.sum(
             jnp.where(ids[k : k + 1, :] == expert, mine, 0.0), axis=0, keepdims=True
         )
-
-    @pl.when(step == pl.num_programs(0) - 1)
-    def _():
-        out_ref[...] = sum_ref[...].astype(BF)
-        gg_ref[...] = part_ref[:top, :] / gates_ref[...].astype(F32)
+        gg_ref[k : k + 1, :] = part / gates_ref[k : k + 1, :].astype(F32)
 
 
 def whole(shape):
@@ -199,7 +190,7 @@
         ],
         out_specs=split((slots // blocks, message)),
         out_shape=jax.ShapeDtypeStruct((slots, message), BF),
-        compiler_params=limits(48),
+        compiler_params=limits(60),
         name="pack_rows",
     )(ids_t, gates_t, tokens, cotangent)
 
@@ -214,8 +205,8 @@
     rows = slots // blocks
     piece = width // LOW
     reply = width + piece + 128
-    gate_t, up_t, down = (
-        pltpu.with_memory_space_constraint(w, pltpu.VMEM) for w in (gate_t, up_t, down)
+    gate_t, up_t, down, held = (
+        pltpu.with_memory_space_constraint(w, pltpu.VMEM) for w in (gate_t, up_t, down, got)
     )
     weight = pl.BlockSpec(memory_space=pltpu.VMEM)
     units = pl.BlockSpec((hidden, rows), lambda b: (0, b))
@@ -223,9 +214,7 @@
         unit_kernel,
         grid=(blocks,),
         in_specs=[
-            split((rows, message)),
-            pl.BlockSpec((slots, 2 * piece), lambda b: (0, LOW)),
-            weight, weight, weight,
+            weight, weight, weight, weight,
         ],
         out_specs=[split((rows, reply))]
         + [units] * 3
@@ -236,9 +225,9 @@
         + [jax.ShapeDtypeStruct((hidden, devices), BF)] * 3
         + [jax.ShapeDtypeStruct((devices, width), BF)] * 2,
         scratch_shapes=[pltpu.VMEM((slots, piece + 128), BF)],
-        compiler_params=limits(48),
+        compiler_params=limits(36),
         name="unit_terms",
-    )(got, got, gate_t, up_t, down)
+    )(held, gate_t, up_t, down)
 
     returned = lax.all_to_all(
         term.reshape(devices, LOW, reply), AXES, split_axis=0, concat_axis=0, tiled=True
@@ -250,20 +239,18 @@
     grad_gate, grad_up = jnp.swapaxes(grad_gate, 0, 1), jnp.swapaxes(grad_up, 0, 1)
     grad_down = (dot(act, dy8) + dot(act9, dy9)).astype(BF)
 
-    blocks = 4
+    held = pltpu.with_memory_space_constraint(returned, pltpu.VMEM)
     grad_tokens, grad_gates = pl.pallas_call(
         lambda *refs: collect_kernel(halves, *refs),
-        grid=(blocks,),
-        in_specs=[whole((top, count)), whole((top, count)), split((slots // blocks, reply))],
-        out_specs=[whole((count, width)), whole((top, count))],
+        in_specs=[pl.BlockSpec(memory_space=pltpu.VMEM)] * 3,
+        out_specs=[pl.BlockSpec(memory_space=pltpu.VMEM)] * 2,
         out_shape=[
             jax.ShapeDtypeStruct((count, width), BF),
             jax.ShapeDtypeStruct((top, count), F32),
         ],
-        scratch_shapes=[pltpu.VMEM((count, width), F32), pltpu.VMEM((8, count), F32)],
-        compiler_params=limits(48),
+        compiler_params=pltpu.CompilerParams(vmem_limit_bytes=32 * 2**20),
         name="collect_rows",
-    )(ids_t, gates_t, returned)
+    )(ids_t, gates_t, held)
     grad_gates = jnp.swapaxes(grad_gates, 0, 1)
     return grad_tokens, grad_gates, grad_gate[None], grad_up[None], grad_down[None]
 

time: 234 us -> 228 us (0.974)
  local copies, waits for them, and re-layouts: 3.34 us -> 0.07 us
    pallas_call x2, Pallas kernels: 33.1 us -> 29.6 us  [the longest x1 24.4 us: local(): pl.pallas_call(unit_kernel, grid=(blocks,), in_specs=[weight, weight, wei...]
    unnamed x40 -> x28, local copies, waits for them, and re-layouts: 3.34 us -> 0.07 us
where the time goes in v3:
time: 228 us
  blocking collectives  122 us (54%)
  waiting for transfers between devices  43.4 us (19%)
  Pallas kernels  36.6 us (16%)
  matrix products  18.8 us (8%)
  starting transfers between devices  6.92 us (3%)
    all_to_all x1, blocking collectives, local(): lax.all_to_all(sent.reshape(devices, LOW, message), AXES, split_axis=0, c...  122 us
    all_to_all x1, waiting for transfers between devices, local(): lax.all_to_all(term.reshape(devices, LOW, reply), AXES, split_axis=0, con...  43.4 us
    pallas_call x1, Pallas kernels, local(): pl.pallas_call(unit_kernel, grid=(blocks,), in_specs=[weight, weight, wei...  24.4 us
    dot_general x6, matrix products, dot(): return lax.dot_general(a, b, dims, preferred_element_type=F32)  18.8 us
    pallas_call x1, Pallas kernels, local(): pl.pallas_call(lambda *refs: pack_kernel(halves, *refs), grid=(blocks,),...  6.98 us
    all_to_all x1, starting transfers between devices, local(): lax.all_to_all(term.reshape(devices, LOW, reply), AXES, split_axis=0, con...  6.92 us
    pallas_call x1, Pallas kernels, local(): pl.pallas_call(lambda *refs: collect_kernel(halves, *refs), in_specs=[pl....  5.24 us
  transfers between devices with their start and end apart: 1, of which 1 were waited for; matrix products, arithmetic and copies ran while one was open for 8% of the time, Pallas kernels for 0%

profile of v3, /device:TPU:8, one launch (start us, length us, event | category | flops | bytes accessed | tf_op | source)
XLA Modules:
  0.0 228.1 jit_solution(14697856358739972228)
XLA Ops:
  0.6 7.0 %pack_rows.1 = bf16[1024,4608]{1,0:T(8,128)(2,1)} custom-call(s32[6,64]{1,0:T(8,128)} %bitcast.38, bf16[6,64]{1,0:T(8,128)(2,1)} %bitcast.40, bf16[64,2048]{1,0:T(8,128)(2,1)} %refs_2_.1, bf16[64,2048]{1,0:T(8,128)(2,1)} %refs_3_.1), custom_call_target="tpu_custom_call" | custom-call | tf_op jit(solution)/shard_map/pack_rows/pallas_call | solution.py:185
  7.6 121.5 %all_to_all.10 = bf16[128,8,4608]{2,1,0:T(8,128)(2,1)S(1)} all-to-all(bf16[128,8,4608]{2,1,0:T(8,128)(2,1)} %bitcast.42), channel_id=1, replica_groups=mesh['node'=8,'local'=16] {'node','local'}, dimensions={0} | all-to-all | bytes 18874368 | tf_op jit(solution)/shard_map/all_to_all | solution.py:197
  129.1 0.0 copy-done.1
  129.1 0.0 copy-done.2
  129.2 0.0 copy-done.3
  129.2 24.4 %unit_terms.1 = (bf16[1024,2432]{1,0:T(8,128)(2,1)}, bf16[704,1024]{1,0:T(8,128)(2,1)}, bf16[704,1024]{1,0:T(8,128)(2,1)}, bf16[704,1024]{1,0:T(8,128)(2,1)}, bf...) custom-call(bf16[1024,4608]{1,0:T(8,128)(2,1)S(1)} %bitcast.29, ...), custom_call_target="tpu_custom_call" | custom-call | tf_op jit(solution)/shard_map/unit_terms/pallas_call | solution.py:213
  153.5 0.0 copy-done
  153.5 0.0 copy-start.10
  153.5 0.0 slice-start
  153.6 6.9 %all-to-all-start.1 = ((bf16[128,8,2432]{2,1,0:T(8,128)(2,1)}), bf16[128,8,2432]{2,1,0:T(8,128)(2,1)}, u32[]{:S(2)}, u32[]{:S(2)}) async-start(bf16[128,8,2432]{2,1,0:T(8,128)(2,1)} %bitcast.43), calls=%async_computation.1 | async-start | bytes 9961472 | tf_op jit(solution)/shard_map/all_to_all | solution.py:232
  160.5 0.0 copy-done.10
  160.5 0.0 copy-start.6
  160.5 0.0 slice-start.1
  160.5 0.0 slice-start.2
  160.5 5.1 %fusion.2 = f32[2048,704]{0,1:T(8,128)S(1)} fusion(bf16[704,1024]{1,0:T(8,128)(2,1)S(1)} %copy-done.10, bf16[1024,4608]{1,0:T(8,128)(2,1)} %bitcast.30), kind=kOutput, calls=%fused_computation.5 | convolution fusion | flops 2952790016 | bytes 11403264 | tf_op jit(solution)/shard_map/dot_general | solution.py:17
  165.6 0.0 copy-done.6
  165.6 0.0 copy-start.9
  165.6 2.5 %fusion.6 = bf16[1,2048,704]{1,2,0:T(8,128)(2,1)} fusion(f32[2048,704]{0,1:T(8,128)S(1)} %fusion.2, bf16[704,128]{1,0:T(8,128)(2,1)S(1)} %get-tuple-element.21, bf16[128,2048]{1,0:T(8,128)(2,1)S(1)} %copy-done.6), kind=kOutput, calls=%fused_computation.9 | convolution fusion | flops 371982336 | bytes 9355264 | tf_op jit(solution)/shard_map/dot_general | solution.py:17
  168.1 0.0 slice-done
  168.1 0.0 slice-done.1
  168.1 0.0 slice-done.2
  168.1 0.0 copy-done.9
  168.1 3.1 %fusion.4 = f32[2048,704]{0,1:T(8,128)S(1)} fusion(bf16[704,1024]{1,0:T(8,128)(2,1)S(1)} %copy-done.9, bf16[1024,4608]{1,0:T(8,128)(2,1)S(1)} %bitcast.33), kind=kOutput, calls=%fused_computation.7 | convolution fusion | flops 2952790016 | bytes 11403264 | tf_op jit(solution)/shard_map/dot_general | solution.py:17
  171.3 2.5 %fusion.7 = bf16[1,2048,704]{1,2,0:T(8,128)(2,1)} fusion(f32[2048,704]{0,1:T(8,128)S(1)} %fusion.4, bf16[704,128]{1,0:T(8,128)(2,1)S(1)} %get-tuple-element.23, bf16[128,2048]{1,0:T(8,128)(2,1)S(1)} %copy-done.6), kind=kOutput, calls=%fused_computation.10 | convolution fusion | flops 371982336 | bytes 9355264 | tf_op jit(solution)/shard_map/dot_general | solution.py:17
  173.8 0.0 copy-done.8
  173.8 3.1 %fusion = f32[704,2048]{1,0:T(8,128)S(1)} fusion(bf16[704,1024]{1,0:T(8,128)(2,1)S(1)} %copy-done.8, bf16[1024,4608]{1,0:T(8,128)(2,1)S(1)} %bitcast.34), kind=kOutput, calls=%fused_computation.3 | convolution fusion | flops 2952790016 | bytes 11403264 | tf_op jit(solution)/shard_map/dot_general | solution.py:17
  176.9 0.0 copy-done.7
  176.9 0.0 copy-start.4
  176.9 0.0 copy-start.5
  177.0 2.5 %fusion.8 = bf16[1,704,2048]{2,1,0:T(8,128)(2,1)} fusion(f32[704,2048]{1,0:T(8,128)S(1)} %fusion, bf16[704,128]{1,0:T(8,128)(2,1)S(1)} %get-tuple-element.25, bf16[128,2048]{1,0:T(8,128)(2,1)S(1)} %copy-done.7), kind=kOutput, calls=%fused_computation.11 | convolution fusion | flops 371982336 | bytes 9355264 | tf_op jit(solution)/shard_map/dot_general | solution.py:17
  179.4 43.4 %all-to-all-done.1 = bf16[128,8,2432]{2,1,0:T(8,128)(2,1)} async-done(((bf16[128,8,2432]{2,1,0:T(8,128)(2,1)}), bf16[128,8,2432]{2,1,0:T(8,128)(2,1)}, u32[]{:S(2)}, u32[]{:S(2)}) %all-to-all-start.1) | async-done | bytes 4980768 | tf_op jit(solution)/shard_map/all_to_all | solution.py:232
  222.9 5.2 %collect_rows.1 = (bf16[64,2048]{1,0:T(8,128)(2,1)}, f32[6,64]{1,0:T(8,128)}) custom-call(s32[6,64]{1,0:T(8,128)S(1)} %bitcast.39, bf16[6,64]{1,0:T(8,128)(2,1)S(1)} %bitcast.41, bf16[1024,2432]{1,0:T(8,128)(2,1)} %bitcast.10.refs_2_), custom_call_target="tpu_custom_call" | custom-call | tf_op jit(solution)/shard_map/collect_rows/pallas_call | solution.py:243
  (9 shorter events, 0.0 us)
Async XLA Ops:
  7.6 121.5 %copy-start.1 = (bf16[1,2048,704]{1,2,0:T(8,128)(2,1)S(1)}, bf16[1,2048,704]{1,2,0:T(8,128)(2,1)}, u32[]{:S(2)}) copy-start(bf16[1,2048,704]{1,2,0:T(8,128)(2,1)} %param.11) | copy-start | bytes 8650756
  7.6 121.5 %copy-start.2 = (bf16[1,2048,704]{1,2,0:T(8,128)(2,1)S(1)}, bf16[1,2048,704]{1,2,0:T(8,128)(2,1)}, u32[]{:S(2)}) copy-start(bf16[1,2048,704]{1,2,0:T(8,128)(2,1)} %param.12) | copy-start | bytes 8650756
  7.6 121.5 %copy-start.3 = (bf16[1,704,2048]{2,1,0:T(8,128)(2,1)S(1)}, bf16[1,704,2048]{2,1,0:T(8,128)(2,1)}, u32[]{:S(2)}) copy-start(bf16[1,704,2048]{2,1,0:T(8,128)(2,1)} %param.13) | copy-start | bytes 8650756
  129.1 24.4 %copy-start = (bf16[128,8,4608]{2,1,0:T(8,128)(2,1)}, bf16[128,8,4608]{2,1,0:T(8,128)(2,1)S(1)}, u32[]{:S(2)}) copy-start(bf16[128,8,4608]{2,1,0:T(8,128)(2,1)S(1)} %all_to_all.10) | copy-start | bytes 28311556
  153.5 7.0 %copy-start.10 = (bf16[704,1024]{1,0:T(8,128)(2,1)S(1)}, bf16[704,1024]{1,0:T(8,128)(2,1)}, u32[]{:S(2)}) copy-start(bf16[704,1024]{1,0:T(8,128)(2,1)} %get-tuple-element.19) | copy-start | bytes 4325380
  153.5 14.6 %slice-start = ((s8[9437184]{0:T(1024)(128)(4,1)}), s8[1048576]{0:T(1024)(128)(4,1)S(1)}, s32[]{:S(2)}) async-start(s8[9437184]{0:T(1024)(128)(4,1)} %bitcast.31), calls=%async_computation.2 | async-start | bytes 2097152
  153.6 69.3 %all-to-all-start.1 = ((bf16[128,8,2432]{2,1,0:T(8,128)(2,1)}), bf16[128,8,2432]{2,1,0:T(8,128)(2,1)}, u32[]{:S(2)}, u32[]{:S(2)}) async-start(bf16[128,8,2432]{2,1,0:T(8,128)(2,1)} %bitcast.43), calls=%async_computation.1 | async-start | bytes 9961472 | tf_op jit(solution)/shard_map/all_to_all | solution.py:232
  160.5 5.1 %copy-start.6 = (bf16[128,2048]{1,0:T(8,128)(2,1)S(1)}, bf16[128,2048]{1,0:T(8,128)(2,1)}, u32[]{:S(2)}) copy-start(bf16[128,2048]{1,0:T(8,128)(2,1)} %get-tuple-element.20) | copy-start | bytes 1572868
  160.5 7.6 %slice-start.1 = ((s8[9437184]{0:T(1024)(128)(4,1)}), s8[4194304]{0:T(1024)(128)(4,1)S(1)}, s32[]{:S(2)}) async-start(s8[9437184]{0:T(1024)(128)(4,1)} %bitcast.31), calls=%async_computation.3 | async-start | bytes 8388608
  160.5 7.6 %slice-start.2 = ((s8[9437184]{0:T(1024)(128)(4,1)}), s8[4194304]{0:T(1024)(128)(4,1)S(1)}, s32[]{:S(2)}) async-start(s8[9437184]{0:T(1024)(128)(4,1)} %bitcast.31), calls=%async_computation.4 | async-start | bytes 8388608
  165.6 2.5 %copy-start.9 = (bf16[704,1024]{1,0:T(8,128)(2,1)S(1)}, bf16[704,1024]{1,0:T(8,128)(2,1)}, u32[]{:S(2)}) copy-start(bf16[704,1024]{1,0:T(8,128)(2,1)} %get-tuple-element.22) | copy-start | bytes 4325380
  171.3 2.5 %copy-start.8 = (bf16[704,1024]{1,0:T(8,128)(2,1)S(1)}, bf16[704,1024]{1,0:T(8,128)(2,1)}, u32[]{:S(2)}) copy-start(bf16[704,1024]{1,0:T(8,128)(2,1)} %get-tuple-element.24) | copy-start | bytes 4325380
  173.8 3.1 %copy-start.7 = (bf16[128,2048]{1,0:T(8,128)(2,1)S(1)}, bf16[128,2048]{1,0:T(8,128)(2,1)}, u32[]{:S(2)}) copy-start(bf16[128,2048]{1,0:T(8,128)(2,1)} %get-tuple-element.26) | copy-start | bytes 1572868
  176.9 45.9 %copy-start.4 = (s32[64,6]{0,1:T(8,128)S(1)}, s32[64,6]{0,1:T(8,128)}, u32[]{:S(2)}) copy-start(s32[64,6]{0,1:T(8,128)} %param.10) | copy-start | bytes 4612
  176.9 45.9 %copy-start.5 = (bf16[64,6]{0,1:T(8,128)(2,1)S(1)}, bf16[64,6]{0,1:T(8,128)(2,1)}, u32[]{:S(2)}) copy-start(bf16[64,6]{0,1:T(8,128)(2,1)} %param.9) | copy-start | bytes 2308

commit v4 on v2

--- a/solution.py
+++ b/solution.py
@@ -65,93 +65,123 @@
     return jnp.where((a % sources) * LOW + a // sources == b, 1.0, 0.0).astype(BF)
 
 
-def nine_rows(got9_ref, rows9):
+def nine_rows(got_ref, at, rows9):
     block = 32
     table = piece_table(block)
     x9, dy9 = [], []
     for first in range(0, rows9, block):
-        pieces = dot(table, got9_ref[first * LOW : (first + block) * LOW, :]).astype(BF)
+        pieces = dot(table, got_ref[first * LOW : (first + block) * LOW, at:]).astype(BF)
         pieces = [pieces[i * block : (i + 1) * block] for i in range(LOW)]
         x9.append(jnp.concatenate(pieces[: LOW // 2], 1))
         dy9.append(jnp.concatenate(pieces[LOW // 2 :], 1))
     return jnp.concatenate(x9, 0), jnp.concatenate(dy9, 0)
 
 
-def unit_rows(x, dy, gate_ref, up_ref, down_ref, dg_ref, du_ref, act_ref):
-    pre_gate = dot(gate_ref[...], x, NT)
-    pre_up = dot(up_ref[...], x, NT)
-    back = dot(down_ref[...], dy, NT)
-    sig = jax.nn.sigmoid(pre_gate)
-    silu = pre_gate * sig
-    act = silu * pre_up
-    part = jnp.sum(act * back, axis=0, keepdims=True)
-    d_gate = (back * pre_up * sig * (1.0 + pre_gate * (1.0 - sig))).astype(BF)
-    d_up = (back * silu).astype(BF)
-    dg_ref[...], du_ref[...], act_ref[...] = d_gate, d_up, act.astype(BF)
-    term = dot(d_gate, gate_ref[...], TN) + dot(d_up, up_ref[...], TN)
-    return term.astype(BF), jnp.transpose(jnp.broadcast_to(part, (128, part.shape[1])))
-
-
 def unit_kernel(
-    got_ref, got9_ref, gate_ref, up_ref, down_ref,
-    back_ref, dg_ref, du_ref, act_ref, dg9_ref, du9_ref, act9_ref, x9_ref, dy9_ref, tail_ref,
+    got_ref, gate_ref, up_ref, down_ref,
+    back_hbm, dg_hbm, du_hbm, act_hbm, dg9_ref, du9_ref, act9_ref, x9_ref, dy9_ref,
+    back_ref, dg_ref, du_ref, act_ref, done,
 ):
-    rows, width = got_ref.shape[0], gate_ref.shape[1]
-    rows9 = x9_ref.shape[0]
+    width = gate_ref.shape[1]
+    blocks, _, rows = dg_ref.shape
+    sources = x9_ref.shape[0]
     piece = width // LOW
+    tail = width + piece
+    copies = []
+
+    def send(source, target):
+        copy = pltpu.make_async_copy(source, target, done.at[len(copies)])
+        copy.start()
+        copies.append(copy)
+
+    def activations(x, dy):
+        pre_gate = dot(gate_ref[...], x, NT)
+        pre_up = dot(up_ref[...], x, NT)
+        back = dot(down_ref[...], dy, NT)
+        sig = jax.nn.sigmoid(pre_gate)
+        silu = pre_gate * sig
+        act = silu * pre_up
+        part = jnp.sum(act * back, axis=0, keepdims=True)
+        d_gate = (back * pre_up * (sig + silu * (1.0 - sig))).astype(BF)
+        d_up = (back * silu).astype(BF)
+        part = jnp.transpose(jnp.broadcast_to(part, (128, part.shape[1])))
+        return d_gate, d_up, act.astype(BF), part
+
+    def terms(d_gate, d_up):
+        return (dot(d_gate, gate_ref[...], TN) + dot(d_up, up_ref[...], TN)).astype(BF)
+
+    def start_block(i):
+        at = slice(i * rows, (i + 1) * rows)
+        d_gate, d_up, act, part = activations(got_ref[at, :width], got_ref[at, width : 2 * width])
+        for held, out, value in (
+            (dg_ref, dg_hbm, d_gate), (du_ref, du_hbm, d_up), (act_ref, act_hbm, act),
+        ):
+            held[i] = value
+            send(held.at[i], out.at[:, pl.ds(i * rows, rows)])
+        lane = lax.broadcasted_iota(jnp.int32, (rows, 128), 1)
+        back_ref[at, tail:] = jnp.where(lane == 0, part, 0.0).astype(BF)
+        return d_gate, d_up
+
+    def end_block(i, d_gate, d_up):
+        back_ref[i * rows : (i + 1) * rows, :width] = terms(d_gate, d_up)
+        here = (pl.ds(i * rows, rows), pl.ds(0, width))
+        send(back_ref.at[here], back_hbm.at[here])
+
+    last = start_block(0)
+    for i in range(1, blocks):
+        now = start_block(i)
+        end_block(i - 1, *last)
+        last = now
+
+    x9, dy9 = nine_rows(got_ref, 2 * width, sources)
+    x9_ref[...], dy9_ref[...] = x9, dy9
+    d_gate, d_up, act, part = activations(x9, dy9)
+    dg9_ref[...], du9_ref[...], act9_ref[...] = d_gate, d_up, act
+    end_block(blocks - 1, *last)
+    term = terms(d_gate, d_up)
     block = 32
-    step = pl.program_id(0)
-
-    @pl.when(step == 0)
-    def _():
-        x9, dy9 = nine_rows(got9_ref, rows9)
-        x9_ref[...], dy9_ref[...] = x9, dy9
-        term, part = unit_rows(x9, dy9, gate_ref, up_ref, down_ref, dg9_ref, du9_ref, act9_ref)
-        table = piece_table(block)
-        lane = lax.broadcasted_iota(jnp.int32, (block, 128), 1)
-        for first in range(0, rows9, block):
-            at = slice(first, first + block)
-            to = slice(first * LOW, (first + block) * LOW)
-            pieces = [term[at, i * piece : (i + 1) * piece] for i in range(LOW)]
-            tail_ref[to, :piece] = dot(table, jnp.concatenate(pieces, 0), TN).astype(BF)
-            part9 = jnp.where(lane == 1, part[at], 0.0).astype(BF)
-            tail_ref[to, piece:] = dot(table[:block], part9, TN).astype(BF)
-
-    term, part = unit_rows(
-        got_ref[:, :width], got_ref[:, width : 2 * width],
-        gate_ref, up_ref, down_ref, dg_ref, du_ref, act_ref,
-    )
-    here = pl.ds(pl.multiple_of(step * rows, rows), rows)
-    back_ref[:, :width] = term
-    back_ref[:, width : width + piece] = tail_ref[here, :piece]
-    lane = lax.broadcasted_iota(jnp.int32, (rows, 128), 1)
-    back_ref[:, width + piece :] = jnp.where(
-        lane == 0, part, tail_ref[here, piece:].astype(F32)
-    ).astype(BF)
+    table = piece_table(block)
+    lane = lax.broadcasted_iota(jnp.int32, (block, 128), 1)
+    for first in range(0, sources, block):
+        at = slice(first, first + block)
+        to = slice(first * LOW, (first + block) * LOW)
+        pieces = [term[at, i * piece : (i + 1) * piece] for i in range(LOW)]
+        back_ref[to, width:tail] = dot(table, jnp.concatenate(pieces, 0), TN).astype(BF)
+        part9 = jnp.where(lane == 1, part[at], 0.0).astype(BF)
+        part9 = dot(table[:block], part9, TN)
+        back_ref[to, tail:] = (back_ref[to, tail:].astype(F32) + part9).astype(BF)
+    here = (slice(None), pl.ds(width, piece + 128))
+    send(back_ref.at[here], back_hbm.at[here])
+    for copy in copies:
+        copy.wait()
 
 
 def collect_kernel(halves, ids_ref, gates_ref, back_ref, out_ref, gg_ref, sum_ref, part_ref):
     rows, width = back_ref.shape[0], out_ref.shape[1]
     step = pl.program_id(0)
     ids = ids_ref[...]
-    top = ids.shape[0]
+    top, count = ids.shape
     first = step * (rows // (halves * LOW))
     expert, row, hit, rank = row_tables(ids, first, rows, halves)
     low = jnp.where(rank == row, hit, 0.0)
     last = jnp.where(rank == LOW, hit, 0.0)
+    piece = width // LOW
 
     @pl.when(step == 0)
     def _():
         sum_ref[...] = jnp.zeros_like(sum_ref)
         part_ref[...] = jnp.zeros_like(part_ref)
 
-    piece = width // LOW
-    pieces = back_ref[:, width : width + piece]
-    total = dot(low.astype(BF), back_ref[:, :width], TN)
+    low_t, last_t = jnp.transpose(low), jnp.transpose(last)
+    row_t = lax.broadcasted_iota(jnp.int32, (count, rows), 1) % LOW
+    masks = jnp.concatenate(
+        [jnp.where(row_t == i, last_t, 0.0).astype(BF) for i in range(LOW)], 0
+    )
+    pieces = dot(masks, back_ref[:, width : width + piece])
+    total = dot(low_t.astype(BF), back_ref[:, :width])
     for i in range(LOW):
-        mask = jnp.where(row == i, last, 0.0).astype(BF)
         at = slice(i * piece, (i + 1) * piece)
-        sum_ref[:, at] += total[:, at] + dot(mask, pieces, TN)
+        sum_ref[:, at] += total[:, at] + pieces[i * count : (i + 1) * count]
     parts = back_ref[:, width + piece :].astype(F32)
     mine = low * parts[:, 0:1] + jnp.where(row == 0, last, 0.0) * parts[:, 1:2]
     for k in range(top):
@@ -199,7 +229,7 @@
         ],
         out_specs=split((slots // blocks, message)),
         out_shape=jax.ShapeDtypeStruct((slots, message), BF),
-        compiler_params=limits(48),
+        compiler_params=limits(60),
         name="pack_rows",
     )(ids_t, gates_t, tokens, cotangent)
 
@@ -210,35 +240,29 @@
     gate_t = jnp.swapaxes(gate_proj[0], 0, 1)
     up_t = jnp.swapaxes(up_proj[0], 0, 1)
     down = down_proj[0]
-    blocks = 2
+    blocks = 4
     rows = slots // blocks
     piece = width // LOW
     reply = width + piece + 128
-    gate_t, up_t, down = (
-        pltpu.with_memory_space_constraint(w, pltpu.VMEM) for w in (gate_t, up_t, down)
-    )
-    weight = pl.BlockSpec(memory_space=pltpu.VMEM)
-    units = pl.BlockSpec((hidden, rows), lambda b: (0, b))
+    gate_t, up_t, down, held = (
+        pltpu.with_memory_space_constraint(w, pltpu.VMEM) for w in (gate_t, up_t, down, got)
+    )
+    inside = pl.BlockSpec(memory_space=pltpu.VMEM)
+    outside = pl.BlockSpec(memory_space=pl.ANY)
     term, d_gate, d_up, act, d_gate9, d_up9, act9, x9, dy9 = pl.pallas_call(
         unit_kernel,
-        grid=(blocks,),
-        in_specs=[
-            split((rows, message)),
-            pl.BlockSpec((slots, 2 * piece), lambda b: (0, LOW)),
-            weight, weight, weight,
-        ],
-        out_specs=[split((rows, reply))]
-        + [units] * 3
-        + [whole((hidden, devices))] * 3
-        + [whole((devices, width))] * 2,
+        in_specs=[inside] * 4,
+        out_specs=[outside] * 4 + [inside] * 5,
         out_shape=[jax.ShapeDtypeStruct((slots, reply), BF)]
         + [jax.ShapeDtypeStruct((hidden, slots), BF)] * 3
         + [jax.ShapeDtypeStruct((hidden, devices), BF)] * 3
         + [jax.ShapeDtypeStruct((devices, width), BF)] * 2,
-        scratch_shapes=[pltpu.VMEM((slots, piece + 128), BF)],
-        compiler_params=limits(48),
+        scratch_shapes=[pltpu.VMEM((slots, reply), BF)]
+        + [pltpu.VMEM((blocks, hidden, rows), BF)] * 3
+        + [pltpu.SemaphoreType.DMA((4 * blocks + 1,))],
+        compiler_params=pltpu.CompilerParams(vmem_limit_bytes=40 * 2**20),
         name="unit_terms",
-    )(got, got, gate_t, up_t, down)
+    )(held, gate_t, up_t, down)
 
     returned = lax.all_to_all(
         term.reshape(devices, LOW, reply), AXES, split_axis=0, concat_axis=0, tiled=True
@@ -250,7 +274,7 @@
     grad_gate, grad_up = jnp.swapaxes(grad_gate, 0, 1), jnp.swapaxes(grad_up, 0, 1)
     grad_down = (dot(act, dy8) + dot(act9, dy9)).astype(BF)
 
-    blocks = 4
+    blocks = 2
     grad_tokens, grad_gates = pl.pallas_call(
         lambda *refs: collect_kernel(halves, *refs),
         grid=(blocks,),

time: 234 us -> 226 us (0.966)
  Pallas kernels: 38.9 us -> 34.2 us
  local copies, waits for them, and re-layouts: 3.34 us -> 0.08 us
    pallas_call x1, Pallas kernels: 27.3 us -> 22.6 us  [local(): pl.pallas_call(unit_kernel, in_specs=[inside] * 4, out_specs=[outside] *...]
    unnamed x40 -> x34, local copies, waits for them, and re-layouts: 3.34 us -> 0.08 us
where the time goes in v4:
time: 226 us
  blocking collectives  122 us (54%)
  waiting for transfers between devices  43.4 us (19%)
  Pallas kernels  34.2 us (15%)
  matrix products  18.8 us (8%)
  starting transfers between devices  6.91 us (3%)
    all_to_all x1, blocking collectives, local(): lax.all_to_all(sent.reshape(devices, LOW, message), AXES, split_axis=0, c...  122 us
    all_to_all x1, waiting for transfers between devices, local(): lax.all_to_all(term.reshape(devices, LOW, reply), AXES, split_axis=0, con...  43.4 us
    pallas_call x1, Pallas kernels, local(): pl.pallas_call(unit_kernel, in_specs=[inside] * 4, out_specs=[outside] *...  22.6 us
    dot_general x6, matrix products, dot(): return lax.dot_general(a, b, dims, preferred_element_type=F32)  18.8 us
    pallas_call x1, Pallas kernels, local(): pl.pallas_call(lambda *refs: pack_kernel(halves, *refs), grid=(blocks,),...  6.99 us
    all_to_all x1, starting transfers between devices, local(): lax.all_to_all(term.reshape(devices, LOW, reply), AXES, split_axis=0, con...  6.91 us
    pallas_call x1, Pallas kernels, local(): pl.pallas_call(lambda *refs: collect_kernel(halves, *refs), grid=(blocks,...  4.56 us
  transfers between devices with their start and end apart: 1, of which 1 were waited for; matrix products, arithmetic and copies ran while one was open for 8% of the time, Pallas kernels for 0%

profile of v4, /device:TPU:8, one launch (start us, length us, event | category | flops | bytes accessed | tf_op | source)
XLA Modules:
  0.0 225.7 jit_solution(5945089756045902164)
XLA Ops:
  0.6 7.0 %pack_rows.1 = bf16[1024,4608]{1,0:T(8,128)(2,1)} custom-call(s32[6,64]{1,0:T(8,128)} %bitcast.38, bf16[6,64]{1,0:T(8,128)(2,1)} %bitcast.40, bf16[64,2048]{1,0:T(8,128)(2,1)} %refs_2_.1, bf16[64,2048]{1,0:T(8,128)(2,1)} %refs_3_.1), custom_call_target="tpu_custom_call" | custom-call | tf_op jit(solution)/shard_map/pack_rows/pallas_call | solution.py:224
  7.6 121.5 %all_to_all.10 = bf16[128,8,4608]{2,1,0:T(8,128)(2,1)S(1)} all-to-all(bf16[128,8,4608]{2,1,0:T(8,128)(2,1)} %bitcast.42), channel_id=1, replica_groups=mesh['node'=8,'local'=16] {'node','local'}, dimensions={0} | all-to-all | bytes 18874368 | tf_op jit(solution)/shard_map/all_to_all | solution.py:236
  129.2 0.0 copy-done.1
  129.2 0.0 copy-done.2
  129.2 0.0 copy-done.3
  129.2 22.6 %unit_terms.1 = (bf16[1024,2432]{1,0:T(8,128)(2,1)}, bf16[704,1024]{1,0:T(8,128)(2,1)}, bf16[704,1024]{1,0:T(8,128)(2,1)}, bf16[704,1024]{1,0:T(8,128)(2,1)}, bf...) custom-call(bf16[1024,4608]{1,0:T(8,128)(2,1)S(1)} %bitcast.29, ...), custom_call_target="tpu_custom_call" | custom-call | tf_op jit(solution)/shard_map/unit_terms/pallas_call | solution.py:252
  151.8 0.0 copy-done
  151.8 0.0 copy-start.13
  151.8 0.0 slice-start
  151.8 6.9 %all-to-all-start.1 = ((bf16[128,8,2432]{2,1,0:T(8,128)(2,1)}), bf16[128,8,2432]{2,1,0:T(8,128)(2,1)}, u32[]{:S(2)}, u32[]{:S(2)}) async-start(bf16[128,8,2432]{2,1,0:T(8,128)(2,1)} %bitcast.43), calls=%async_computation.1 | async-start | bytes 9961472 | tf_op jit(solution)/shard_map/all_to_all | solution.py:267
  158.8 0.0 copy-done.13
  158.8 0.0 copy-start.6
  158.8 0.0 copy-start.10
  158.8 0.0 slice-start.1
  158.8 0.0 slice-start.2
  158.8 5.1 %fusion.2 = f32[2048,704]{0,1:T(8,128)S(1)} fusion(bf16[704,1024]{1,0:T(8,128)(2,1)S(1)} %copy-done.13, bf16[1024,4608]{1,0:T(8,128)(2,1)} %bitcast.30), kind=kOutput, calls=%fused_computation.5 | convolution fusion | flops 2952790016 | bytes 11403264 | tf_op jit(solution)/shard_map/dot_general | solution.py:17
  163.9 0.0 copy-done.6
  163.9 0.0 copy-start.12
  164.0 2.5 %fusion.6 = bf16[1,2048,704]{1,2,0:T(8,128)(2,1)} fusion(f32[2048,704]{0,1:T(8,128)S(1)} %fusion.2, bf16[704,128]{1,0:T(8,128)(2,1)S(1)} %copy-done.10, bf16[128,2048]{1,0:T(8,128)(2,1)S(1)} %copy-done.6), kind=kOutput, calls=%fused_computation.9 | convolution fusion | flops 371982336 | bytes 9355264 | tf_op jit(solution)/shard_map/dot_general | solution.py:17
  166.4 0.0 slice-done.2
  166.5 3.1 %fusion.4 = f32[2048,704]{0,1:T(8,128)S(1)} fusion(bf16[704,1024]{1,0:T(8,128)(2,1)S(1)} %copy-done.12, bf16[1024,4608]{1,0:T(8,128)(2,1)S(1)} %bitcast.33), kind=kOutput, calls=%fused_computation.7 | convolution fusion | flops 2952790016 | bytes 11403264 | tf_op jit(solution)/shard_map/dot_general | solution.py:17
  169.6 2.5 %fusion.7 = bf16[1,2048,704]{1,2,0:T(8,128)(2,1)} fusion(f32[2048,704]{0,1:T(8,128)S(1)} %fusion.4, bf16[704,128]{1,0:T(8,128)(2,1)S(1)} %copy-done.9, bf16[128,2048]{1,0:T(8,128)(2,1)S(1)} %copy-done.6), kind=kOutput, calls=%fused_computation.10 | convolution fusion | flops 371982336 | bytes 9355264 | tf_op jit(solution)/shard_map/dot_general | solution.py:17
  172.1 0.0 copy-done.11
  172.1 3.1 %fusion = f32[704,2048]{1,0:T(8,128)S(1)} fusion(bf16[704,1024]{1,0:T(8,128)(2,1)S(1)} %copy-done.11, bf16[1024,4608]{1,0:T(8,128)(2,1)S(1)} %bitcast.34), kind=kOutput, calls=%fused_computation.3 | convolution fusion | flops 2952790016 | bytes 11403264 | tf_op jit(solution)/shard_map/dot_general | solution.py:17
  175.3 0.0 copy-done.7
  175.3 0.0 copy-done.8
  175.3 0.0 copy-start.4
  175.3 0.0 copy-start.5
  175.3 2.5 %fusion.8 = bf16[1,704,2048]{2,1,0:T(8,128)(2,1)} fusion(f32[704,2048]{1,0:T(8,128)S(1)} %fusion, bf16[704,128]{1,0:T(8,128)(2,1)S(1)} %copy-done.8, bf16[128,2048]{1,0:T(8,128)(2,1)S(1)} %copy-done.7), kind=kOutput, calls=%fused_computation.11 | convolution fusion | flops 371982336 | bytes 9355264 | tf_op jit(solution)/shard_map/dot_general | solution.py:17
  177.8 43.4 %all-to-all-done.1 = bf16[128,8,2432]{2,1,0:T(8,128)(2,1)} async-done(((bf16[128,8,2432]{2,1,0:T(8,128)(2,1)}), bf16[128,8,2432]{2,1,0:T(8,128)(2,1)}, u32[]{:S(2)}, u32[]{:S(2)}) %all-to-all-start.1) | async-done | bytes 4980768 | tf_op jit(solution)/shard_map/all_to_all | solution.py:267
  221.2 0.0 copy-done.4
  221.2 4.6 %collect_rows.1 = (bf16[64,2048]{1,0:T(8,128)(2,1)}, f32[6,64]{1,0:T(8,128)}) custom-call(s32[6,64]{1,0:T(8,128)S(1)} %bitcast.39, bf16[6,64]{1,0:T(8,128)(2,1)S(1)} %bitcast.41, bf16[1024,2432]{1,0:T(8,128)(2,1)} %bitcast.10.refs_2_), custom_call_target="tpu_custom_call" | custom-call | tf_op jit(solution)/shard_map/collect_rows/pallas_call | solution.py:278
  (15 shorter events, 0.0 us)
Async XLA Ops:
  7.6 121.5 %copy-start.1 = (bf16[1,2048,704]{1,2,0:T(8,128)(2,1)S(1)}, bf16[1,2048,704]{1,2,0:T(8,128)(2,1)}, u32[]{:S(2)}) copy-start(bf16[1,2048,704]{1,2,0:T(8,128)(2,1)} %param.11) | copy-start | bytes 8650756
  7.6 121.5 %copy-start.2 = (bf16[1,2048,704]{1,2,0:T(8,128)(2,1)S(1)}, bf16[1,2048,704]{1,2,0:T(8,128)(2,1)}, u32[]{:S(2)}) copy-start(bf16[1,2048,704]{1,2,0:T(8,128)(2,1)} %param.12) | copy-start | bytes 8650756
  7.6 121.5 %copy-start.3 = (bf16[1,704,2048]{2,1,0:T(8,128)(2,1)S(1)}, bf16[1,704,2048]{2,1,0:T(8,128)(2,1)}, u32[]{:S(2)}) copy-start(bf16[1,704,2048]{2,1,0:T(8,128)(2,1)} %param.13) | copy-start | bytes 8650756
  129.2 22.7 %copy-start = (bf16[128,8,4608]{2,1,0:T(8,128)(2,1)}, bf16[128,8,4608]{2,1,0:T(8,128)(2,1)S(1)}, u32[]{:S(2)}) copy-start(bf16[128,8,4608]{2,1,0:T(8,128)(2,1)S(1)} %all_to_all.10) | copy-start | bytes 28311556
  151.8 6.9 %copy-start.13 = (bf16[704,1024]{1,0:T(8,128)(2,1)S(1)}, bf16[704,1024]{1,0:T(8,128)(2,1)}, u32[]{:S(2)}) copy-start(bf16[704,1024]{1,0:T(8,128)(2,1)} %get-tuple-element.19) | copy-start | bytes 4325380
  151.8 14.6 %slice-start = ((s8[9437184]{0:T(1024)(128)(4,1)}), s8[1048576]{0:T(1024)(128)(4,1)S(1)}, s32[]{:S(2)}) async-start(s8[9437184]{0:T(1024)(128)(4,1)} %bitcast.31), calls=%async_computation.2 | async-start | bytes 2097152
  151.8 69.3 %all-to-all-start.1 = ((bf16[128,8,2432]{2,1,0:T(8,128)(2,1)}), bf16[128,8,2432]{2,1,0:T(8,128)(2,1)}, u32[]{:S(2)}, u32[]{:S(2)}) async-start(bf16[128,8,2432]{2,1,0:T(8,128)(2,1)} %bitcast.43), calls=%async_computation.1 | async-start | bytes 9961472 | tf_op jit(solution)/shard_map/all_to_all | solution.py:267
  158.8 5.1 %copy-start.6 = (bf16[128,2048]{1,0:T(8,128)(2,1)S(1)}, bf16[128,2048]{1,0:T(8,128)(2,1)}, u32[]{:S(2)}) copy-start(bf16[128,2048]{1,0:T(8,128)(2,1)} %get-tuple-element.20) | copy-start | bytes 1572868
  158.8 5.1 %copy-start.10 = (bf16[704,128]{1,0:T(8,128)(2,1)S(1)}, bf16[704,128]{1,0:T(8,128)(2,1)}, u32[]{:S(2)}) copy-start(bf16[704,128]{1,0:T(8,128)(2,1)} %get-tuple-element.21) | copy-start | bytes 540676
  158.8 7.6 %slice-start.1 = ((s8[9437184]{0:T(1024)(128)(4,1)}), s8[4194304]{0:T(1024)(128)(4,1)S(1)}, s32[]{:S(2)}) async-start(s8[9437184]{0:T(1024)(128)(4,1)} %bitcast.31), calls=%async_computation.3 | async-start | bytes 8388608
  158.8 7.6 %slice-start.2 = ((s8[9437184]{0:T(1024)(128)(4,1)}), s8[4194304]{0:T(1024)(128)(4,1)S(1)}, s32[]{:S(2)}) async-start(s8[9437184]{0:T(1024)(128)(4,1)} %bitcast.31), calls=%async_computation.4 | async-start | bytes 8388608
  163.9 2.5 %copy-start.12 = (bf16[704,1024]{1,0:T(8,128)(2,1)S(1)}, bf16[704,1024]{1,0:T(8,128)(2,1)}, u32[]{:S(2)}) copy-start(bf16[704,1024]{1,0:T(8,128)(2,1)} %get-tuple-element.22) | copy-start | bytes 4325380
  166.5 3.2 %copy-start.9 = (bf16[704,128]{1,0:T(8,128)(2,1)S(1)}, bf16[704,128]{1,0:T(8,128)(2,1)}, u32[]{:S(2)}) copy-start(bf16[704,128]{1,0:T(8,128)(2,1)} %get-tuple-element.23) | copy-start | bytes 540676
  169.6 2.5 %copy-start.11 = (bf16[704,1024]{1,0:T(8,128)(2,1)S(1)}, bf16[704,1024]{1,0:T(8,128)(2,1)}, u32[]{:S(2)}) copy-start(bf16[704,1024]{1,0:T(8,128)(2,1)} %get-tuple-element.24) | copy-start | bytes 4325380
  172.1 3.1 %copy-start.7 = (bf16[128,2048]{1,0:T(8,128)(2,1)S(1)}, bf16[128,2048]{1,0:T(8,128)(2,1)}, u32[]{:S(2)}) copy-start(bf16[128,2048]{1,0:T(8,128)(2,1)} %get-tuple-element.26) | copy-start | bytes 1572868
  172.1 3.2 %copy-start.8 = (bf16[704,128]{1,0:T(8,128)(2,1)S(1)}, bf16[704,128]{1,0:T(8,128)(2,1)}, u32[]{:S(2)}) copy-start(bf16[704,128]{1,0:T(8,128)(2,1)} %get-tuple-element.25) | copy-start | bytes 540676
  175.3 45.9 %copy-start.4 = (s32[64,6]{0,1:T(8,128)S(1)}, s32[64,6]{0,1:T(8,128)}, u32[]{:S(2)}) copy-start(s32[64,6]{0,1:T(8,128)} %param.10) | copy-start | bytes 4612
  175.3 45.9 %copy-start.5 = (bf16[64,6]{0,1:T(8,128)(2,1)S(1)}, bf16[64,6]{0,1:T(8,128)(2,1)}, u32[]{:S(2)}) copy-start(bf16[64,6]{0,1:T(8,128)(2,1)} %param.9) | copy-start | bytes 2308

commit v5 on v4

--- a/solution.py
+++ b/solution.py
@@ -9,6 +9,7 @@
 BF = jnp.bfloat16
 F32 = jnp.float32
 AXES = ("node", "local")
+ORDER = ("local", "node")
 NT = (((1,), (1,)), ((), ()))
 TN = (((0,), (0,)), ((), ()))
 
@@ -17,11 +18,17 @@
     return lax.dot_general(a, b, dims, preferred_element_type=F32)
 
 
-def row_tables(ids, first, rows, halves):
+def over(a, n):
+    assert n & (n - 1) == 0
+    return lax.shift_right_logical(a, n.bit_length() - 1), a & (n - 1)
+
+
+def row_tables(ids, first, rows, sizes):
     tokens = ids.shape[1]
-    slot = lax.broadcasted_iota(jnp.int32, (rows, tokens), 0)
-    expert = first + slot // (halves * LOW)
-    row = slot % LOW
+    nodes, members, halves = sizes
+    device, row = over(first + lax.broadcasted_iota(jnp.int32, (rows, 1), 0), LOW)
+    unit, node = over(device, nodes)
+    expert = node * members + over(unit, halves)[0]
     hit = jnp.zeros((rows, tokens), F32)
     for k in range(ids.shape[0]):
         hit = hit + jnp.where(ids[k : k + 1, :] == expert, 1.0, 0.0)
@@ -32,19 +39,19 @@
     return expert, row, hit, rank
 
 
-def pack_kernel(halves, ids_ref, gates_ref, x_ref, dy_ref, out_ref):
-    rows, width = out_ref.shape[0], x_ref.shape[1]
+def pack_kernel(sizes, ids_ref, gates_ref, x_ref, dy_ref, out_ref):
+    nodes, members, halves = sizes
+    width = x_ref.shape[1]
+    run = nodes * LOW
+    rows = out_ref.shape[0] // halves
     ids = ids_ref[...]
     gates = gates_ref[...].astype(F32)
-    first = pl.program_id(0) * (rows // (halves * LOW))
-    expert, row, hit, rank = row_tables(ids, first, rows, halves)
+    expert, row, hit, rank = row_tables(ids, pl.program_id(0) * rows, rows, (nodes, members, 1))
     gate = jnp.zeros(hit.shape, F32)
     for k in range(ids.shape[0]):
         gate = gate + jnp.where(ids[k : k + 1, :] == expert, gates[k : k + 1, :], 0.0)
     low = jnp.where(rank == row, hit, 0.0)
     x, dy = x_ref[...], dy_ref[...]
-    out_ref[:, :width] = dot(low.astype(BF), x).astype(BF)
-    out_ref[:, width : 2 * width] = dot((low * gate).astype(BF), dy).astype(BF)
     last = jnp.where(rank == LOW, hit, 0.0)
     piece = 2 * width // LOW
     masks, pieces = [], []
@@ -53,16 +60,26 @@
         source, weight = (x, last) if at < width else (dy, last * gate)
         masks.append(jnp.where(row == i, weight, 0.0).astype(BF))
         pieces.append(source[:, at % width : at % width + piece])
-    out_ref[:, 2 * width :] = dot(
-        jnp.concatenate(masks, 1), jnp.concatenate(pieces, 0)
-    ).astype(BF)
+
+    def put(value, to):
+        value = value.astype(BF)
+        for i in range(rows // run):
+            for half in range(halves):
+                first = (i * halves + half) * run
+                out_ref[first : first + run, to] = value[i * run : (i + 1) * run]
+
+    put(dot(low.astype(BF), x), slice(0, width))
+    put(dot((low * gate).astype(BF), dy), slice(width, 2 * width))
+    nine = dot(jnp.concatenate(masks, 1), jnp.concatenate(pieces, 0))
+    put(nine, slice(2 * width, 2 * width + piece))
 
 
 def piece_table(sources):
     shape = (sources * LOW, sources * LOW)
     a = lax.broadcasted_iota(jnp.int32, shape, 0)
     b = lax.broadcasted_iota(jnp.int32, shape, 1)
-    return jnp.where((a % sources) * LOW + a // sources == b, 1.0, 0.0).astype(BF)
+    piece, source = over(a, sources)
+    return jnp.where(source * LOW + piece == b, 1.0, 0.0).astype(BF)
 
 
 def nine_rows(got_ref, at, rows9):
@@ -156,13 +173,13 @@
         copy.wait()
 
 
-def collect_kernel(halves, ids_ref, gates_ref, back_ref, out_ref, gg_ref, sum_ref, part_ref):
+def collect_kernel(sizes, ids_ref, gates_ref, back_ref, out_ref, gg_ref, sum_ref, part_ref):
     rows, width = back_ref.shape[0], out_ref.shape[1]
     step = pl.program_id(0)
     ids = ids_ref[...]
     top, count = ids.shape
-    first = step * (rows // (halves * LOW))
-    expert, row, hit, rank = row_tables(ids, first, rows, halves)
+    first = step * rows
+    expert, row, hit, rank = row_tables(ids, first, rows, sizes)
     low = jnp.where(rank == row, hit, 0.0)
     last = jnp.where(rank == LOW, hit, 0.0)
     piece = width // LOW
@@ -173,7 +190,7 @@
         part_ref[...] = jnp.zeros_like(part_ref)
 
     low_t, last_t = jnp.transpose(low), jnp.transpose(last)
-    row_t = lax.broadcasted_iota(jnp.int32, (count, rows), 1) % LOW
+    row_t = over(lax.broadcasted_iota(jnp.int32, (1, rows), 1), LOW)[1]
     masks = jnp.concatenate(
         [jnp.where(row_t == i, last_t, 0.0).astype(BF) for i in range(LOW)], 0
     )
@@ -210,11 +227,12 @@
 
 
 def local(tokens, cotangent, gate_weights, expert_ids, gate_proj, up_proj, down_proj):
-    devices = lax.axis_size("node") * lax.axis_size("local")
+    nodes, locals_ = lax.axis_size("node"), lax.axis_size("local")
+    devices = nodes * locals_
     count, width = tokens.shape
     hidden = down_proj.shape[1]
     halves = 2
-    experts = devices // halves
+    sizes = (nodes, locals_ // halves, halves)
     slots = devices * LOW
     top = expert_ids.shape[1]
     ids_t, gates_t = jnp.swapaxes(expert_ids, 0, 1), jnp.swapaxes(gate_weights, 0, 1)
@@ -222,7 +240,7 @@
     blocks = 4
     message = 2 * width + 2 * width // LOW
     sent = pl.pallas_call(
-        lambda *refs: pack_kernel(halves, *refs),
+        lambda *refs: pack_kernel(sizes, *refs),
         grid=(blocks,),
         in_specs=[
             whole((top, count)), whole((top, count)), whole((count, width)), whole((count, width)),
@@ -234,7 +252,7 @@
     )(ids_t, gates_t, tokens, cotangent)
 
     got = lax.all_to_all(
-        sent.reshape(devices, LOW, message), AXES, split_axis=0, concat_axis=0, tiled=True
+        sent.reshape(devices, LOW, message), ORDER, split_axis=0, concat_axis=0, tiled=True
     ).reshape(slots, message)
 
     gate_t = jnp.swapaxes(gate_proj[0], 0, 1)
@@ -265,7 +283,7 @@
     )(held, gate_t, up_t, down)
 
     returned = lax.all_to_all(
-        term.reshape(devices, LOW, reply), AXES, split_axis=0, concat_axis=0, tiled=True
+        term.reshape(devices, LOW, reply), ORDER, split_axis=0, concat_axis=0, tiled=True
     ).reshape(slots, reply)
 
     x8, dy8 = got[:, :width], got[:, width : 2 * width]
@@ -276,7 +294,7 @@
 
     blocks = 2
     grad_tokens, grad_gates = pl.pallas_call(
-        lambda *refs: collect_kernel(halves, *refs),
+        lambda *refs: collect_kernel(sizes, *refs),
         grid=(blocks,),
         in_specs=[whole((top, count)), whole((top, count)), split((slots // blocks, reply))],
         out_specs=[whole((count, width)), whole((top, count))],

time: 226 us -> 223 us (0.987)
  blocking collectives: 122 us -> 119 us
    all_to_all x1, blocking collectives: 122 us -> 119 us  [local(): lax.all_to_all(sent.reshape(devices, LOW, message), ORDER, split_axis=0,...]
  transfers between devices with their start and end apart: 1 -> 1, of which waited for: 1 -> 1; matrix products, arithmetic and copies ran while one was open for 8% -> 9% of each run, Pallas kernels for 0% -> 0%
where the time goes in v5:
time: 223 us; the launch traced here: 221 us
  blocking collectives  119 us (53%)
  waiting for transfers between devices  41.2 us (18%)
  Pallas kernels  33.3 us (15%)
  matrix products  18.8 us (8%)
  starting transfers between devices  8.1 us (4%)
    all_to_all x1, blocking collectives, local(): lax.all_to_all(sent.reshape(devices, LOW, message), ORDER, split_axis=0,...  119 us
    all_to_all x1, waiting for transfers between devices, local(): lax.all_to_all(term.reshape(devices, LOW, reply), ORDER, split_axis=0, co...  41.2 us
    pallas_call x1, Pallas kernels, local(): pl.pallas_call(unit_kernel, in_specs=[inside] * 4, out_specs=[outside] *...  22.6 us
    dot_general x6, matrix products, dot(): return lax.dot_general(a, b, dims, preferred_element_type=F32)  18.8 us
    all_to_all x1, starting transfers between devices, local(): lax.all_to_all(term.reshape(devices, LOW, reply), ORDER, split_axis=0, co...  8.1 us
    pallas_call x1, Pallas kernels, local(): pl.pallas_call(lambda *refs: pack_kernel(sizes, *refs), grid=(blocks,), i...  5.99 us
    pallas_call x1, Pallas kernels, local(): pl.pallas_call(lambda *refs: collect_kernel(sizes, *refs), grid=(blocks,)...  4.65 us
  transfers between devices with their start and end apart: 1, of which 1 were waited for; matrix products, arithmetic and copies ran while one was open for 9% of the time, Pallas kernels for 0%

profile of v5, /device:TPU:8, one launch (start us, length us, event | category | flops | bytes accessed | tf_op | source)
XLA Modules:
  0.0 221.0 jit_solution(16298218685006996861)
XLA Ops:
  0.6 6.0 %pack_rows.1 = bf16[1024,4608]{1,0:T(8,128)(2,1)} custom-call(s32[6,64]{1,0:T(8,128)} %bitcast.38, bf16[6,64]{1,0:T(8,128)(2,1)} %bitcast.40, bf16[64,2048]{1,0:T(8,128)(2,1)} %refs_2_.1, bf16[64,2048]{1,0:T(8,128)(2,1)} %refs_3_.1), custom_call_target="tpu_custom_call" | custom-call | tf_op jit(solution)/shard_map/pack_rows/pallas_call | solution.py:242
  6.6 118.7 %all_to_all.10 = bf16[128,8,4608]{2,1,0:T(8,128)(2,1)S(1)} all-to-all(bf16[128,8,4608]{2,1,0:T(8,128)(2,1)} %bitcast.42), channel_id=1, replica_groups=mesh['node'=8,'local'=16] {'local','node'}, dimensions={0} | all-to-all | bytes 18874368 | tf_op jit(solution)/shard_map/all_to_all | solution.py:254
  125.4 0.0 copy-done.1
  125.4 0.0 copy-done.2
  125.4 0.0 copy-done.3
  125.4 22.6 %unit_terms.1 = (bf16[1024,2432]{1,0:T(8,128)(2,1)}, bf16[704,1024]{1,0:T(8,128)(2,1)}, bf16[704,1024]{1,0:T(8,128)(2,1)}, bf16[704,1024]{1,0:T(8,128)(2,1)}, bf...) custom-call(bf16[1024,4608]{1,0:T(8,128)(2,1)S(1)} %bitcast.29, ...), custom_call_target="tpu_custom_call" | custom-call | tf_op jit(solution)/shard_map/unit_terms/pallas_call | solution.py:270
  148.0 0.0 copy-done
  148.0 0.0 copy-start.13
  148.0 0.0 slice-start
  148.1 8.1 %all-to-all-start.1 = ((bf16[128,8,2432]{2,1,0:T(8,128)(2,1)}), bf16[128,8,2432]{2,1,0:T(8,128)(2,1)}, u32[]{:S(2)}, u32[]{:S(2)}) async-start(bf16[128,8,2432]{2,1,0:T(8,128)(2,1)} %bitcast.43), calls=%async_computation.1 | async-start | bytes 9961472 | tf_op jit(solution)/shard_map/all_to_all | solution.py:285
  156.2 0.0 copy-done.13
  156.2 0.0 copy-start.6
  156.2 0.0 copy-start.10
  156.2 0.0 slice-start.1
  156.2 0.0 slice-start.2
  156.2 5.1 %fusion.2 = f32[2048,704]{0,1:T(8,128)S(1)} fusion(bf16[704,1024]{1,0:T(8,128)(2,1)S(1)} %copy-done.13, bf16[1024,4608]{1,0:T(8,128)(2,1)} %bitcast.30), kind=kOutput, calls=%fused_computation.5 | convolution fusion | flops 2952790016 | bytes 11403264 | tf_op jit(solution)/shard_map/dot_general | solution.py:18
  161.3 0.0 copy-done.6
  161.3 0.0 copy-done.10
  161.3 0.0 copy-start.12
  161.3 2.5 %fusion.6 = bf16[1,2048,704]{1,2,0:T(8,128)(2,1)} fusion(f32[2048,704]{0,1:T(8,128)S(1)} %fusion.2, bf16[704,128]{1,0:T(8,128)(2,1)S(1)} %copy-done.10, bf16[128,2048]{1,0:T(8,128)(2,1)S(1)} %copy-done.6), kind=kOutput, calls=%fused_computation.9 | convolution fusion | flops 371982336 | bytes 9355264 | tf_op jit(solution)/shard_map/dot_general | solution.py:18
  163.8 0.0 slice-done
  163.8 0.0 slice-done.2
  163.9 3.1 %fusion.4 = f32[2048,704]{0,1:T(8,128)S(1)} fusion(bf16[704,1024]{1,0:T(8,128)(2,1)S(1)} %copy-done.12, bf16[1024,4608]{1,0:T(8,128)(2,1)S(1)} %bitcast.33), kind=kOutput, calls=%fused_computation.7 | convolution fusion | flops 2952790016 | bytes 11403264 | tf_op jit(solution)/shard_map/dot_general | solution.py:18
  167.0 2.5 %fusion.7 = bf16[1,2048,704]{1,2,0:T(8,128)(2,1)} fusion(f32[2048,704]{0,1:T(8,128)S(1)} %fusion.4, bf16[704,128]{1,0:T(8,128)(2,1)S(1)} %copy-done.9, bf16[128,2048]{1,0:T(8,128)(2,1)S(1)} %copy-done.6), kind=kOutput, calls=%fused_computation.10 | convolution fusion | flops 371982336 | bytes 9355264 | tf_op jit(solution)/shard_map/dot_general | solution.py:18
  169.5 0.0 copy-done.11
  169.5 3.1 %fusion = f32[704,2048]{1,0:T(8,128)S(1)} fusion(bf16[704,1024]{1,0:T(8,128)(2,1)S(1)} %copy-done.11, bf16[1024,4608]{1,0:T(8,128)(2,1)S(1)} %bitcast.34), kind=kOutput, calls=%fused_computation.3 | convolution fusion | flops 2952790016 | bytes 11403264 | tf_op jit(solution)/shard_map/dot_general | solution.py:18
  172.7 0.0 copy-start.4
  172.7 0.0 copy-start.5
  172.7 2.5 %fusion.8 = bf16[1,704,2048]{2,1,0:T(8,128)(2,1)} fusion(f32[704,2048]{1,0:T(8,128)S(1)} %fusion, bf16[704,128]{1,0:T(8,128)(2,1)S(1)} %copy-done.8, bf16[128,2048]{1,0:T(8,128)(2,1)S(1)} %copy-done.7), kind=kOutput, calls=%fused_computation.11 | convolution fusion | flops 371982336 | bytes 9355264 | tf_op jit(solution)/shard_map/dot_general | solution.py:18
  175.2 41.2 %all-to-all-done.1 = bf16[128,8,2432]{2,1,0:T(8,128)(2,1)} async-done(((bf16[128,8,2432]{2,1,0:T(8,128)(2,1)}), bf16[128,8,2432]{2,1,0:T(8,128)(2,1)}, u32[]{:S(2)}, u32[]{:S(2)}) %all-to-all-start.1) | async-done | bytes 4980768 | tf_op jit(solution)/shard_map/all_to_all | solution.py:285
  216.3 0.0 copy-done.5
  216.3 4.7 %collect_rows.1 = (bf16[64,2048]{1,0:T(8,128)(2,1)}, f32[6,64]{1,0:T(8,128)}) custom-call(s32[6,64]{1,0:T(8,128)S(1)} %bitcast.39, bf16[6,64]{1,0:T(8,128)(2,1)S(1)} %bitcast.41, bf16[1024,2432]{1,0:T(8,128)(2,1)} %bitcast.10.refs_2_), custom_call_target="tpu_custom_call" | custom-call | tf_op jit(solution)/shard_map/collect_rows/pallas_call | solution.py:296
  (15 shorter events, 0.0 us)
Async XLA Ops:
  6.6 118.7 %copy-start.1 = (bf16[1,2048,704]{1,2,0:T(8,128)(2,1)S(1)}, bf16[1,2048,704]{1,2,0:T(8,128)(2,1)}, u32[]{:S(2)}) copy-start(bf16[1,2048,704]{1,2,0:T(8,128)(2,1)} %param.11) | copy-start | bytes 8650756
  6.6 118.7 %copy-start.2 = (bf16[1,2048,704]{1,2,0:T(8,128)(2,1)S(1)}, bf16[1,2048,704]{1,2,0:T(8,128)(2,1)}, u32[]{:S(2)}) copy-start(bf16[1,2048,704]{1,2,0:T(8,128)(2,1)} %param.12) | copy-start | bytes 8650756
  6.6 118.7 %copy-start.3 = (bf16[1,704,2048]{2,1,0:T(8,128)(2,1)S(1)}, bf16[1,704,2048]{2,1,0:T(8,128)(2,1)}, u32[]{:S(2)}) copy-start(bf16[1,704,2048]{2,1,0:T(8,128)(2,1)} %param.13) | copy-start | bytes 8650756
  125.4 22.7 %copy-start = (bf16[128,8,4608]{2,1,0:T(8,128)(2,1)}, bf16[128,8,4608]{2,1,0:T(8,128)(2,1)S(1)}, u32[]{:S(2)}) copy-start(bf16[128,8,4608]{2,1,0:T(8,128)(2,1)S(1)} %all_to_all.10) | copy-start | bytes 28311556
  148.0 8.1 %copy-start.13 = (bf16[704,1024]{1,0:T(8,128)(2,1)S(1)}, bf16[704,1024]{1,0:T(8,128)(2,1)}, u32[]{:S(2)}) copy-start(bf16[704,1024]{1,0:T(8,128)(2,1)} %get-tuple-element.19) | copy-start | bytes 4325380
  148.0 15.8 %slice-start = ((s8[9437184]{0:T(1024)(128)(4,1)}), s8[1048576]{0:T(1024)(128)(4,1)S(1)}, s32[]{:S(2)}) async-start(s8[9437184]{0:T(1024)(128)(4,1)} %bitcast.31), calls=%async_computation.2 | async-start | bytes 2097152
  148.1 68.3 %all-to-all-start.1 = ((bf16[128,8,2432]{2,1,0:T(8,128)(2,1)}), bf16[128,8,2432]{2,1,0:T(8,128)(2,1)}, u32[]{:S(2)}, u32[]{:S(2)}) async-start(bf16[128,8,2432]{2,1,0:T(8,128)(2,1)} %bitcast.43), calls=%async_computation.1 | async-start | bytes 9961472 | tf_op jit(solution)/shard_map/all_to_all | solution.py:285
  156.2 5.1 %copy-start.6 = (bf16[128,2048]{1,0:T(8,128)(2,1)S(1)}, bf16[128,2048]{1,0:T(8,128)(2,1)}, u32[]{:S(2)}) copy-start(bf16[128,2048]{1,0:T(8,128)(2,1)} %get-tuple-element.20) | copy-start | bytes 1572868
  156.2 5.1 %copy-start.10 = (bf16[704,128]{1,0:T(8,128)(2,1)S(1)}, bf16[704,128]{1,0:T(8,128)(2,1)}, u32[]{:S(2)}) copy-start(bf16[704,128]{1,0:T(8,128)(2,1)} %get-tuple-element.21) | copy-start | bytes 540676
  156.2 7.6 %slice-start.1 = ((s8[9437184]{0:T(1024)(128)(4,1)}), s8[4194304]{0:T(1024)(128)(4,1)S(1)}, s32[]{:S(2)}) async-start(s8[9437184]{0:T(1024)(128)(4,1)} %bitcast.31), calls=%async_computation.3 | async-start | bytes 8388608
  156.2 7.6 %slice-start.2 = ((s8[9437184]{0:T(1024)(128)(4,1)}), s8[4194304]{0:T(1024)(128)(4,1)S(1)}, s32[]{:S(2)}) async-start(s8[9437184]{0:T(1024)(128)(4,1)} %bitcast.31), calls=%async_computation.4 | async-start | bytes 8388608
  161.3 2.5 %copy-start.12 = (bf16[704,1024]{1,0:T(8,128)(2,1)S(1)}, bf16[704,1024]{1,0:T(8,128)(2,1)}, u32[]{:S(2)}) copy-start(bf16[704,1024]{1,0:T(8,128)(2,1)} %get-tuple-element.22) | copy-start | bytes 4325380
  163.8 3.2 %copy-start.9 = (bf16[704,128]{1,0:T(8,128)(2,1)S(1)}, bf16[704,128]{1,0:T(8,128)(2,1)}, u32[]{:S(2)}) copy-start(bf16[704,128]{1,0:T(8,128)(2,1)} %get-tuple-element.23) | copy-start | bytes 540676
  167.0 2.5 %copy-start.11 = (bf16[704,1024]{1,0:T(8,128)(2,1)S(1)}, bf16[704,1024]{1,0:T(8,128)(2,1)}, u32[]{:S(2)}) copy-start(bf16[704,1024]{1,0:T(8,128)(2,1)} %get-tuple-element.24) | copy-start | bytes 4325380
  169.5 3.1 %copy-start.7 = (bf16[128,2048]{1,0:T(8,128)(2,1)S(1)}, bf16[128,2048]{1,0:T(8,128)(2,1)}, u32[]{:S(2)}) copy-start(bf16[128,2048]{1,0:T(8,128)(2,1)} %get-tuple-element.26) | copy-start | bytes 1572868
  169.5 3.2 %copy-start.8 = (bf16[704,128]{1,0:T(8,128)(2,1)S(1)}, bf16[704,128]{1,0:T(8,128)(2,1)}, u32[]{:S(2)}) copy-start(bf16[704,128]{1,0:T(8,128)(2,1)} %get-tuple-element.25) | copy-start | bytes 540676
  172.7 43.7 %copy-start.4 = (s32[64,6]{0,1:T(8,128)S(1)}, s32[64,6]{0,1:T(8,128)}, u32[]{:S(2)}) copy-start(s32[64,6]{0,1:T(8,128)} %param.10) | copy-start | bytes 4612
  172.7 43.7 %copy-start.5 = (bf16[64,6]{0,1:T(8,128)(2,1)S(1)}, bf16[64,6]{0,1:T(8,128)(2,1)}, u32[]{:S(2)}) copy-start(bf16[64,6]{0,1:T(8,128)(2,1)} %param.9) | copy-start | bytes 2308

commit v6 on v5

--- a/solution.py
+++ b/solution.py
@@ -1,3 +1,5 @@
+import math
+
 import jax
 import jax.numpy as jnp
 from jax import lax
@@ -8,8 +10,8 @@
 LOW = 8
 BF = jnp.bfloat16
 F32 = jnp.float32
-AXES = ("node", "local")
-ORDER = ("local", "node")
+AXES = ("node", "y", "z")
+ORDER = ("z", "y", "node")
 NT = (((1,), (1,)), ((), ()))
 TN = (((0,), (0,)), ((), ()))
 
@@ -25,10 +27,11 @@
 
 def row_tables(ids, first, rows, sizes):
     tokens = ids.shape[1]
-    nodes, members, halves = sizes
+    nodes, ys, pairs, halves = sizes
     device, row = over(first + lax.broadcasted_iota(jnp.int32, (rows, 1), 0), LOW)
     unit, node = over(device, nodes)
-    expert = node * members + over(unit, halves)[0]
+    z, y = over(unit, ys)
+    expert = (node * ys + y) * pairs + over(z, halves)[0]
     hit = jnp.zeros((rows, tokens), F32)
     for k in range(ids.shape[0]):
         hit = hit + jnp.where(ids[k : k + 1, :] == expert, 1.0, 0.0)
@@ -40,13 +43,13 @@
 
 
 def pack_kernel(sizes, ids_ref, gates_ref, x_ref, dy_ref, out_ref):
-    nodes, members, halves = sizes
+    nodes, ys, pairs, halves = sizes
     width = x_ref.shape[1]
-    run = nodes * LOW
+    run = ys * nodes * LOW
     rows = out_ref.shape[0] // halves
     ids = ids_ref[...]
     gates = gates_ref[...].astype(F32)
-    expert, row, hit, rank = row_tables(ids, pl.program_id(0) * rows, rows, (nodes, members, 1))
+    expert, row, hit, rank = row_tables(ids, pl.program_id(0) * rows, rows, (nodes, ys, pairs, 1))
     gate = jnp.zeros(hit.shape, F32)
     for k in range(ids.shape[0]):
         gate = gate + jnp.where(ids[k : k + 1, :] == expert, gates[k : k + 1, :], 0.0)
@@ -227,17 +230,17 @@
 
 
 def local(tokens, cotangent, gate_weights, expert_ids, gate_proj, up_proj, down_proj):
-    nodes, locals_ = lax.axis_size("node"), lax.axis_size("local")
-    devices = nodes * locals_
+    nodes, ys, zs = (lax.axis_size(name) for name in AXES)
+    devices = nodes * ys * zs
     count, width = tokens.shape
     hidden = down_proj.shape[1]
     halves = 2
-    sizes = (nodes, locals_ // halves, halves)
+    sizes = (nodes, ys, zs // halves, halves)
     slots = devices * LOW
     top = expert_ids.shape[1]
     ids_t, gates_t = jnp.swapaxes(expert_ids, 0, 1), jnp.swapaxes(gate_weights, 0, 1)
 
-    blocks = 4
+    blocks = zs // halves
     message = 2 * width + 2 * width // LOW
     sent = pl.pallas_call(
         lambda *refs: pack_kernel(sizes, *refs),
@@ -311,6 +314,9 @@
 
 
 def solution(mesh):
+    nodes, members = mesh.devices.shape
+    side = math.isqrt(members)
+    mesh = jax.sharding.Mesh(mesh.devices.reshape(nodes, side, members // side), AXES)
     row = P(AXES, None)
     unit = P(AXES, None, None)
     return jax.shard_map(

time: 223 us -> 221 us (level)
  no operation moved by 1% of the time
where the time goes in v6:
time: 221 us; the launch traced here: 219 us
  blocking collectives  119 us (54%)
  waiting for transfers between devices  41.1 us (19%)
  Pallas kernels  33.2 us (15%)
  matrix products  18.8 us (9%)
  starting transfers between devices  6.55 us (3%)
    all_to_all x1, blocking collectives, local(): lax.all_to_all(sent.reshape(devices, LOW, message), ORDER, split_axis=0,...  119 us
    all_to_all x1, waiting for transfers between devices, local(): lax.all_to_all(term.reshape(devices, LOW, reply), ORDER, split_axis=0, co...  41.1 us
    pallas_call x1, Pallas kernels, local(): pl.pallas_call(unit_kernel, in_specs=[inside] * 4, out_specs=[outside] *...  22.6 us
    dot_general x6, matrix products, dot(): return lax.dot_general(a, b, dims, preferred_element_type=F32)  18.8 us
    all_to_all x1, starting transfers between devices, local(): lax.all_to_all(term.reshape(devices, LOW, reply), ORDER, split_axis=0, co...  6.55 us
    pallas_call x1, Pallas kernels, local(): pl.pallas_call(lambda *refs: pack_kernel(sizes, *refs), grid=(blocks,), i...  5.8 us
    pallas_call x1, Pallas kernels, local(): pl.pallas_call(lambda *refs: collect_kernel(sizes, *refs), grid=(blocks,)...  4.73 us
  transfers between devices with their start and end apart: 1, of which 1 were waited for; matrix products, arithmetic and copies ran while one was open for 9% of the time, Pallas kernels for 0%

profile of v6, /device:TPU:8, one launch (start us, length us, event | category | flops | bytes accessed | tf_op | source)
XLA Modules:
  0.0 219.2 jit_solution(2770291892031414422)
XLA Ops:
  0.6 5.8 %pack_rows.1 = bf16[1024,4608]{1,0:T(8,128)(2,1)} custom-call(s32[6,64]{1,0:T(8,128)} %bitcast.38, bf16[6,64]{1,0:T(8,128)(2,1)} %bitcast.40, bf16[64,2048]{1,0:T(8,128)(2,1)} %refs_2_.1, bf16[64,2048]{1,0:T(8,128)(2,1)} %refs_3_.1), custom_call_target="tpu_custom_call" | custom-call | tf_op jit(solution)/shard_map/pack_rows/pallas_call | solution.py:245
  6.4 118.7 %all_to_all.10 = bf16[128,8,4608]{2,1,0:T(8,128)(2,1)S(1)} all-to-all(bf16[128,8,4608]{2,1,0:T(8,128)(2,1)} %bitcast.42), channel_id=1, replica_groups=mesh['node'=8,'y'=4,'z'=4] {'z','y','node'}, dimensions={0} | all-to-all | bytes 18874368 | tf_op jit(solution)/shard_map/all_to_all | solution.py:257
  125.2 0.0 copy-done.1
  125.2 0.0 copy-done.2
  125.2 0.0 copy-done.3
  125.2 22.6 %unit_terms.1 = (bf16[1024,2432]{1,0:T(8,128)(2,1)}, bf16[704,1024]{1,0:T(8,128)(2,1)}, bf16[704,1024]{1,0:T(8,128)(2,1)}, bf16[704,1024]{1,0:T(8,128)(2,1)}, bf...) custom-call(bf16[1024,4608]{1,0:T(8,128)(2,1)S(1)} %bitcast.29, ...), custom_call_target="tpu_custom_call" | custom-call | tf_op jit(solution)/shard_map/unit_terms/pallas_call | solution.py:273
  147.8 0.0 copy-done
  147.8 0.0 copy-start.13
  147.9 0.0 slice-start
  147.9 6.6 %all-to-all-start.1 = ((bf16[128,8,2432]{2,1,0:T(8,128)(2,1)}), bf16[128,8,2432]{2,1,0:T(8,128)(2,1)}, u32[]{:S(2)}, u32[]{:S(2)}) async-start(bf16[128,8,2432]{2,1,0:T(8,128)(2,1)} %bitcast.43), calls=%async_computation.1 | async-start | bytes 9961472 | tf_op jit(solution)/shard_map/all_to_all | solution.py:288
  154.4 0.0 copy-done.13
  154.4 0.0 copy-start.6
  154.4 0.0 copy-start.10
  154.5 0.0 slice-start.1
  154.5 0.0 slice-start.2
  154.5 5.1 %fusion.2 = f32[2048,704]{0,1:T(8,128)S(1)} fusion(bf16[704,1024]{1,0:T(8,128)(2,1)S(1)} %copy-done.13, bf16[1024,4608]{1,0:T(8,128)(2,1)} %bitcast.30), kind=kOutput, calls=%fused_computation.5 | convolution fusion | flops 2952790016 | bytes 11403264 | tf_op jit(solution)/shard_map/dot_general | solution.py:20
  159.6 0.0 copy-done.6
  159.6 0.0 copy-done.10
  159.6 0.0 copy-start.12
  159.6 2.5 %fusion.6 = bf16[1,2048,704]{1,2,0:T(8,128)(2,1)} fusion(f32[2048,704]{0,1:T(8,128)S(1)} %fusion.2, bf16[704,128]{1,0:T(8,128)(2,1)S(1)} %copy-done.10, bf16[128,2048]{1,0:T(8,128)(2,1)S(1)} %copy-done.6), kind=kOutput, calls=%fused_computation.9 | convolution fusion | flops 371982336 | bytes 9355264 | tf_op jit(solution)/shard_map/dot_general | solution.py:20
  162.1 0.0 copy-done.12
  162.1 3.1 %fusion.4 = f32[2048,704]{0,1:T(8,128)S(1)} fusion(bf16[704,1024]{1,0:T(8,128)(2,1)S(1)} %copy-done.12, bf16[1024,4608]{1,0:T(8,128)(2,1)S(1)} %bitcast.33), kind=kOutput, calls=%fused_computation.7 | convolution fusion | flops 2952790016 | bytes 11403264 | tf_op jit(solution)/shard_map/dot_general | solution.py:20
  165.3 2.5 %fusion.7 = bf16[1,2048,704]{1,2,0:T(8,128)(2,1)} fusion(f32[2048,704]{0,1:T(8,128)S(1)} %fusion.4, bf16[704,128]{1,0:T(8,128)(2,1)S(1)} %copy-done.9, bf16[128,2048]{1,0:T(8,128)(2,1)S(1)} %copy-done.6), kind=kOutput, calls=%fused_computation.10 | convolution fusion | flops 371982336 | bytes 9355264 | tf_op jit(solution)/shard_map/dot_general | solution.py:20
  167.8 3.1 %fusion = f32[704,2048]{1,0:T(8,128)S(1)} fusion(bf16[704,1024]{1,0:T(8,128)(2,1)S(1)} %copy-done.11, bf16[1024,4608]{1,0:T(8,128)(2,1)S(1)} %bitcast.34), kind=kOutput, calls=%fused_computation.3 | convolution fusion | flops 2952790016 | bytes 11403264 | tf_op jit(solution)/shard_map/dot_general | solution.py:20
  170.9 0.0 copy-done.7
  170.9 0.0 copy-done.8
  170.9 0.0 copy-start.4
  170.9 0.0 copy-start.5
  170.9 2.5 %fusion.8 = bf16[1,704,2048]{2,1,0:T(8,128)(2,1)} fusion(f32[704,2048]{1,0:T(8,128)S(1)} %fusion, bf16[704,128]{1,0:T(8,128)(2,1)S(1)} %copy-done.8, bf16[128,2048]{1,0:T(8,128)(2,1)S(1)} %copy-done.7), kind=kOutput, calls=%fused_computation.11 | convolution fusion | flops 371982336 | bytes 9355264 | tf_op jit(solution)/shard_map/dot_general | solution.py:20
  173.4 41.1 %all-to-all-done.1 = bf16[128,8,2432]{2,1,0:T(8,128)(2,1)} async-done(((bf16[128,8,2432]{2,1,0:T(8,128)(2,1)}), bf16[128,8,2432]{2,1,0:T(8,128)(2,1)}, u32[]{:S(2)}, u32[]{:S(2)}) %all-to-all-start.1) | async-done | bytes 4980768 | tf_op jit(solution)/shard_map/all_to_all | solution.py:288
  214.5 0.0 copy-done.5
  214.5 4.7 %collect_rows.1 = (bf16[64,2048]{1,0:T(8,128)(2,1)}, f32[6,64]{1,0:T(8,128)}) custom-call(s32[6,64]{1,0:T(8,128)S(1)} %bitcast.39, bf16[6,64]{1,0:T(8,128)(2,1)S(1)} %bitcast.41, bf16[1024,2432]{1,0:T(8,128)(2,1)} %bitcast.10.refs_2_), custom_call_target="tpu_custom_call" | custom-call | tf_op jit(solution)/shard_map/collect_rows/pallas_call | solution.py:299
  (15 shorter events, 0.0 us)
Async XLA Ops:
  6.4 118.7 %copy-start.1 = (bf16[1,2048,704]{1,2,0:T(8,128)(2,1)S(1)}, bf16[1,2048,704]{1,2,0:T(8,128)(2,1)}, u32[]{:S(2)}) copy-start(bf16[1,2048,704]{1,2,0:T(8,128)(2,1)} %param.11) | copy-start | bytes 8650756
  6.4 118.7 %copy-start.2 = (bf16[1,2048,704]{1,2,0:T(8,128)(2,1)S(1)}, bf16[1,2048,704]{1,2,0:T(8,128)(2,1)}, u32[]{:S(2)}) copy-start(bf16[1,2048,704]{1,2,0:T(8,128)(2,1)} %param.12) | copy-start | bytes 8650756
  6.4 118.7 %copy-start.3 = (bf16[1,704,2048]{2,1,0:T(8,128)(2,1)S(1)}, bf16[1,704,2048]{2,1,0:T(8,128)(2,1)}, u32[]{:S(2)}) copy-start(bf16[1,704,2048]{2,1,0:T(8,128)(2,1)} %param.13) | copy-start | bytes 8650756
  125.2 22.7 %copy-start = (bf16[128,8,4608]{2,1,0:T(8,128)(2,1)}, bf16[128,8,4608]{2,1,0:T(8,128)(2,1)S(1)}, u32[]{:S(2)}) copy-start(bf16[128,8,4608]{2,1,0:T(8,128)(2,1)S(1)} %all_to_all.10) | copy-start | bytes 28311556
  147.8 6.6 %copy-start.13 = (bf16[704,1024]{1,0:T(8,128)(2,1)S(1)}, bf16[704,1024]{1,0:T(8,128)(2,1)}, u32[]{:S(2)}) copy-start(bf16[704,1024]{1,0:T(8,128)(2,1)} %get-tuple-element.19) | copy-start | bytes 4325380
  147.9 14.2 %slice-start = ((s8[9437184]{0:T(1024)(128)(4,1)}), s8[1048576]{0:T(1024)(128)(4,1)S(1)}, s32[]{:S(2)}) async-start(s8[9437184]{0:T(1024)(128)(4,1)} %bitcast.31), calls=%async_computation.2 | async-start | bytes 2097152
  147.9 66.6 %all-to-all-start.1 = ((bf16[128,8,2432]{2,1,0:T(8,128)(2,1)}), bf16[128,8,2432]{2,1,0:T(8,128)(2,1)}, u32[]{:S(2)}, u32[]{:S(2)}) async-start(bf16[128,8,2432]{2,1,0:T(8,128)(2,1)} %bitcast.43), calls=%async_computation.1 | async-start | bytes 9961472 | tf_op jit(solution)/shard_map/all_to_all | solution.py:288
  154.4 5.1 %copy-start.6 = (bf16[128,2048]{1,0:T(8,128)(2,1)S(1)}, bf16[128,2048]{1,0:T(8,128)(2,1)}, u32[]{:S(2)}) copy-start(bf16[128,2048]{1,0:T(8,128)(2,1)} %get-tuple-element.20) | copy-start | bytes 1572868
  154.4 5.1 %copy-start.10 = (bf16[704,128]{1,0:T(8,128)(2,1)S(1)}, bf16[704,128]{1,0:T(8,128)(2,1)}, u32[]{:S(2)}) copy-start(bf16[704,128]{1,0:T(8,128)(2,1)} %get-tuple-element.21) | copy-start | bytes 540676
  154.5 7.6 %slice-start.1 = ((s8[9437184]{0:T(1024)(128)(4,1)}), s8[4194304]{0:T(1024)(128)(4,1)S(1)}, s32[]{:S(2)}) async-start(s8[9437184]{0:T(1024)(128)(4,1)} %bitcast.31), calls=%async_computation.3 | async-start | bytes 8388608
  154.5 7.6 %slice-start.2 = ((s8[9437184]{0:T(1024)(128)(4,1)}), s8[4194304]{0:T(1024)(128)(4,1)S(1)}, s32[]{:S(2)}) async-start(s8[9437184]{0:T(1024)(128)(4,1)} %bitcast.31), calls=%async_computation.4 | async-start | bytes 8388608
  159.6 2.5 %copy-start.12 = (bf16[704,1024]{1,0:T(8,128)(2,1)S(1)}, bf16[704,1024]{1,0:T(8,128)(2,1)}, u32[]{:S(2)}) copy-start(bf16[704,1024]{1,0:T(8,128)(2,1)} %get-tuple-element.22) | copy-start | bytes 4325380
  162.1 3.2 %copy-start.9 = (bf16[704,128]{1,0:T(8,128)(2,1)S(1)}, bf16[704,128]{1,0:T(8,128)(2,1)}, u32[]{:S(2)}) copy-start(bf16[704,128]{1,0:T(8,128)(2,1)} %get-tuple-element.23) | copy-start | bytes 540676
  165.3 2.5 %copy-start.11 = (bf16[704,1024]{1,0:T(8,128)(2,1)S(1)}, bf16[704,1024]{1,0:T(8,128)(2,1)}, u32[]{:S(2)}) copy-start(bf16[704,1024]{1,0:T(8,128)(2,1)} %get-tuple-element.24) | copy-start | bytes 4325380
  167.8 3.1 %copy-start.7 = (bf16[128,2048]{1,0:T(8,128)(2,1)S(1)}, bf16[128,2048]{1,0:T(8,128)(2,1)}, u32[]{:S(2)}) copy-start(bf16[128,2048]{1,0:T(8,128)(2,1)} %get-tuple-element.26) | copy-start | bytes 1572868
  167.8 3.2 %copy-start.8 = (bf16[704,128]{1,0:T(8,128)(2,1)S(1)}, bf16[704,128]{1,0:T(8,128)(2,1)}, u32[]{:S(2)}) copy-start(bf16[704,128]{1,0:T(8,128)(2,1)} %get-tuple-element.25) | copy-start | bytes 540676
  170.9 43.6 %copy-start.4 = (s32[64,6]{0,1:T(8,128)S(1)}, s32[64,6]{0,1:T(8,128)}, u32[]{:S(2)}) copy-start(s32[64,6]{0,1:T(8,128)} %param.10) | copy-start | bytes 4612
  170.9 43.6 %copy-start.5 = (bf16[64,6]{0,1:T(8,128)(2,1)S(1)}, bf16[64,6]{0,1:T(8,128)(2,1)}, u32[]{:S(2)}) copy-start(bf16[64,6]{0,1:T(8,128)(2,1)} %param.9) | copy-start | bytes 2308

commit v7 on v6

--- a/solution.py
+++ b/solution.py
@@ -148,7 +148,7 @@
         send(back_ref.at[here], back_hbm.at[here])
 
     last = start_block(0)
-    for i in range(1, blocks):
+    for i in range(1, blocks - 1):
         now = start_block(i)
         end_block(i - 1, *last)
         last = now
@@ -157,7 +157,8 @@
     x9_ref[...], dy9_ref[...] = x9, dy9
     d_gate, d_up, act, part = activations(x9, dy9)
     dg9_ref[...], du9_ref[...], act9_ref[...] = d_gate, d_up, act
-    end_block(blocks - 1, *last)
+    end_block(blocks - 2, *last)
+    last = start_block(blocks - 1)
     term = terms(d_gate, d_up)
     block = 32
     table = piece_table(block)
@@ -172,6 +173,7 @@
         back_ref[to, tail:] = (back_ref[to, tail:].astype(F32) + part9).astype(BF)
     here = (slice(None), pl.ds(width, piece + 128))
     send(back_ref.at[here], back_hbm.at[here])
+    end_block(blocks - 1, *last)
     for copy in copies:
         copy.wait()
 

time: 221 us -> 223 us (level)
  no operation moved by 1% of the time
where the time goes in v7:
time: 223 us; the launch traced here: 220 us
  blocking collectives  119 us (53%)
  waiting for transfers between devices  41.1 us (18%)
  Pallas kernels  34.3 us (15%)
  matrix products  18.8 us (8%)
  starting transfers between devices  6.55 us (3%)
    all_to_all x1, blocking collectives, local(): lax.all_to_all(sent.reshape(devices, LOW, message), ORDER, split_axis=0,...  119 us
    all_to_all x1, waiting for transfers between devices, local(): lax.all_to_all(term.reshape(devices, LOW, reply), ORDER, split_axis=0, co...  41.1 us
    pallas_call x1, Pallas kernels, local(): pl.pallas_call(unit_kernel, in_specs=[inside] * 4, out_specs=[outside] *...  23.8 us
    dot_general x6, matrix products, dot(): return lax.dot_general(a, b, dims, preferred_element_type=F32)  18.8 us
    all_to_all x1, starting transfers between devices, local(): lax.all_to_all(term.reshape(devices, LOW, reply), ORDER, split_axis=0, co...  6.55 us
    pallas_call x1, Pallas kernels, local(): pl.pallas_call(lambda *refs: pack_kernel(sizes, *refs), grid=(blocks,), i...  5.8 us
    pallas_call x1, Pallas kernels, local(): pl.pallas_call(lambda *refs: collect_kernel(sizes, *refs), grid=(blocks,)...  4.73 us
  transfers between devices with their start and end apart: 1, of which 1 were waited for; matrix products, arithmetic and copies ran while one was open for 9% of the time, Pallas kernels for 0%

profile of v7, /device:TPU:8, one launch (start us, length us, event | category | flops | bytes accessed | tf_op | source)
XLA Modules:
  0.0 220.4 jit_solution(15285730799332521827)
XLA Ops:
  0.6 5.8 %pack_rows.1 = bf16[1024,4608]{1,0:T(8,128)(2,1)} custom-call(s32[6,64]{1,0:T(8,128)} %bitcast.38, bf16[6,64]{1,0:T(8,128)(2,1)} %bitcast.40, bf16[64,2048]{1,0:T(8,128)(2,1)} %refs_2_.1, bf16[64,2048]{1,0:T(8,128)(2,1)} %refs_3_.1), custom_call_target="tpu_custom_call" | custom-call | tf_op jit(solution)/shard_map/pack_rows/pallas_call | solution.py:247
  6.4 118.7 %all_to_all.10 = bf16[128,8,4608]{2,1,0:T(8,128)(2,1)S(1)} all-to-all(bf16[128,8,4608]{2,1,0:T(8,128)(2,1)} %bitcast.42), channel_id=1, replica_groups=mesh['node'=8,'y'=4,'z'=4] {'z','y','node'}, dimensions={0} | all-to-all | bytes 18874368 | tf_op jit(solution)/shard_map/all_to_all | solution.py:259
  125.2 0.0 copy-done.1
  125.2 0.0 copy-done.2
  125.2 0.0 copy-done.3
  125.2 23.8 %unit_terms.1 = (bf16[1024,2432]{1,0:T(8,128)(2,1)}, bf16[704,1024]{1,0:T(8,128)(2,1)}, bf16[704,1024]{1,0:T(8,128)(2,1)}, bf16[704,1024]{1,0:T(8,128)(2,1)}, bf...) custom-call(bf16[1024,4608]{1,0:T(8,128)(2,1)S(1)} %bitcast.29, ...), custom_call_target="tpu_custom_call" | custom-call | tf_op jit(solution)/shard_map/unit_terms/pallas_call | solution.py:275
  149.0 0.0 copy-done
  149.0 0.0 copy-start.13
  149.0 0.0 slice-start
  149.0 6.6 %all-to-all-start.1 = ((bf16[128,8,2432]{2,1,0:T(8,128)(2,1)}), bf16[128,8,2432]{2,1,0:T(8,128)(2,1)}, u32[]{:S(2)}, u32[]{:S(2)}) async-start(bf16[128,8,2432]{2,1,0:T(8,128)(2,1)} %bitcast.43), calls=%async_computation.1 | async-start | bytes 9961472 | tf_op jit(solution)/shard_map/all_to_all | solution.py:290
  155.6 0.0 copy-done.13
  155.6 0.0 copy-start.6
  155.6 0.0 copy-start.10
  155.6 0.0 slice-start.1
  155.6 0.0 slice-start.2
  155.7 5.1 %fusion.2 = f32[2048,704]{0,1:T(8,128)S(1)} fusion(bf16[704,1024]{1,0:T(8,128)(2,1)S(1)} %copy-done.13, bf16[1024,4608]{1,0:T(8,128)(2,1)} %bitcast.30), kind=kOutput, calls=%fused_computation.5 | convolution fusion | flops 2952790016 | bytes 11403264 | tf_op jit(solution)/shard_map/dot_general | solution.py:20
  160.8 0.0 copy-done.6
  160.8 0.0 copy-done.10
  160.8 0.0 copy-start.12
  160.8 2.5 %fusion.6 = bf16[1,2048,704]{1,2,0:T(8,128)(2,1)} fusion(f32[2048,704]{0,1:T(8,128)S(1)} %fusion.2, bf16[704,128]{1,0:T(8,128)(2,1)S(1)} %copy-done.10, bf16[128,2048]{1,0:T(8,128)(2,1)S(1)} %copy-done.6), kind=kOutput, calls=%fused_computation.9 | convolution fusion | flops 371982336 | bytes 9355264 | tf_op jit(solution)/shard_map/dot_general | solution.py:20
  163.3 0.0 slice-done.1
  163.3 3.1 %fusion.4 = f32[2048,704]{0,1:T(8,128)S(1)} fusion(bf16[704,1024]{1,0:T(8,128)(2,1)S(1)} %copy-done.12, bf16[1024,4608]{1,0:T(8,128)(2,1)S(1)} %bitcast.33), kind=kOutput, calls=%fused_computation.7 | convolution fusion | flops 2952790016 | bytes 11403264 | tf_op jit(solution)/shard_map/dot_general | solution.py:20
  166.4 0.0 copy-done.9
  166.5 0.0 copy-start.11
  166.5 2.5 %fusion.7 = bf16[1,2048,704]{1,2,0:T(8,128)(2,1)} fusion(f32[2048,704]{0,1:T(8,128)S(1)} %fusion.4, bf16[704,128]{1,0:T(8,128)(2,1)S(1)} %copy-done.9, bf16[128,2048]{1,0:T(8,128)(2,1)S(1)} %copy-done.6), kind=kOutput, calls=%fused_computation.10 | convolution fusion | flops 371982336 | bytes 9355264 | tf_op jit(solution)/shard_map/dot_general | solution.py:20
  168.9 3.1 %fusion = f32[704,2048]{1,0:T(8,128)S(1)} fusion(bf16[704,1024]{1,0:T(8,128)(2,1)S(1)} %copy-done.11, bf16[1024,4608]{1,0:T(8,128)(2,1)S(1)} %bitcast.34), kind=kOutput, calls=%fused_computation.3 | convolution fusion | flops 2952790016 | bytes 11403264 | tf_op jit(solution)/shard_map/dot_general | solution.py:20
  172.1 0.0 copy-start.4
  172.1 0.0 copy-start.5
  172.1 2.5 %fusion.8 = bf16[1,704,2048]{2,1,0:T(8,128)(2,1)} fusion(f32[704,2048]{1,0:T(8,128)S(1)} %fusion, bf16[704,128]{1,0:T(8,128)(2,1)S(1)} %copy-done.8, bf16[128,2048]{1,0:T(8,128)(2,1)S(1)} %copy-done.7), kind=kOutput, calls=%fused_computation.11 | convolution fusion | flops 371982336 | bytes 9355264 | tf_op jit(solution)/shard_map/dot_general | solution.py:20
  174.6 41.1 %all-to-all-done.1 = bf16[128,8,2432]{2,1,0:T(8,128)(2,1)} async-done(((bf16[128,8,2432]{2,1,0:T(8,128)(2,1)}), bf16[128,8,2432]{2,1,0:T(8,128)(2,1)}, u32[]{:S(2)}, u32[]{:S(2)}) %all-to-all-start.1) | async-done | bytes 4980768 | tf_op jit(solution)/shard_map/all_to_all | solution.py:290
  215.7 0.0 copy-done.4
  215.7 4.7 %collect_rows.1 = (bf16[64,2048]{1,0:T(8,128)(2,1)}, f32[6,64]{1,0:T(8,128)}) custom-call(s32[6,64]{1,0:T(8,128)S(1)} %bitcast.39, bf16[6,64]{1,0:T(8,128)(2,1)S(1)} %bitcast.41, bf16[1024,2432]{1,0:T(8,128)(2,1)} %bitcast.10.refs_2_), custom_call_target="tpu_custom_call" | custom-call | tf_op jit(solution)/shard_map/collect_rows/pallas_call | solution.py:301
  (15 shorter events, 0.0 us)
Async XLA Ops:
  6.4 118.7 %copy-start.1 = (bf16[1,2048,704]{1,2,0:T(8,128)(2,1)S(1)}, bf16[1,2048,704]{1,2,0:T(8,128)(2,1)}, u32[]{:S(2)}) copy-start(bf16[1,2048,704]{1,2,0:T(8,128)(2,1)} %param.11) | copy-start | bytes 8650756
  6.4 118.7 %copy-start.2 = (bf16[1,2048,704]{1,2,0:T(8,128)(2,1)S(1)}, bf16[1,2048,704]{1,2,0:T(8,128)(2,1)}, u32[]{:S(2)}) copy-start(bf16[1,2048,704]{1,2,0:T(8,128)(2,1)} %param.12) | copy-start | bytes 8650756
  6.4 118.7 %copy-start.3 = (bf16[1,704,2048]{2,1,0:T(8,128)(2,1)S(1)}, bf16[1,704,2048]{2,1,0:T(8,128)(2,1)}, u32[]{:S(2)}) copy-start(bf16[1,704,2048]{2,1,0:T(8,128)(2,1)} %param.13) | copy-start | bytes 8650756
  125.2 23.8 %copy-start = (bf16[128,8,4608]{2,1,0:T(8,128)(2,1)}, bf16[128,8,4608]{2,1,0:T(8,128)(2,1)S(1)}, u32[]{:S(2)}) copy-start(bf16[128,8,4608]{2,1,0:T(8,128)(2,1)S(1)} %all_to_all.10) | copy-start | bytes 28311556
  149.0 6.6 %copy-start.13 = (bf16[704,1024]{1,0:T(8,128)(2,1)S(1)}, bf16[704,1024]{1,0:T(8,128)(2,1)}, u32[]{:S(2)}) copy-start(bf16[704,1024]{1,0:T(8,128)(2,1)} %get-tuple-element.19) | copy-start | bytes 4325380
  149.0 14.2 %slice-start = ((s8[9437184]{0:T(1024)(128)(4,1)}), s8[1048576]{0:T(1024)(128)(4,1)S(1)}, s32[]{:S(2)}) async-start(s8[9437184]{0:T(1024)(128)(4,1)} %bitcast.31), calls=%async_computation.2 | async-start | bytes 2097152
  149.0 66.6 %all-to-all-start.1 = ((bf16[128,8,2432]{2,1,0:T(8,128)(2,1)}), bf16[128,8,2432]{2,1,0:T(8,128)(2,1)}, u32[]{:S(2)}, u32[]{:S(2)}) async-start(bf16[128,8,2432]{2,1,0:T(8,128)(2,1)} %bitcast.43), calls=%async_computation.1 | async-start | bytes 9961472 | tf_op jit(solution)/shard_map/all_to_all | solution.py:290
  155.6 5.1 %copy-start.6 = (bf16[128,2048]{1,0:T(8,128)(2,1)S(1)}, bf16[128,2048]{1,0:T(8,128)(2,1)}, u32[]{:S(2)}) copy-start(bf16[128,2048]{1,0:T(8,128)(2,1)} %get-tuple-element.20) | copy-start | bytes 1572868
  155.6 5.1 %copy-start.10 = (bf16[704,128]{1,0:T(8,128)(2,1)S(1)}, bf16[704,128]{1,0:T(8,128)(2,1)}, u32[]{:S(2)}) copy-start(bf16[704,128]{1,0:T(8,128)(2,1)} %get-tuple-element.21) | copy-start | bytes 540676
  155.6 7.6 %slice-start.1 = ((s8[9437184]{0:T(1024)(128)(4,1)}), s8[4194304]{0:T(1024)(128)(4,1)S(1)}, s32[]{:S(2)}) async-start(s8[9437184]{0:T(1024)(128)(4,1)} %bitcast.31), calls=%async_computation.3 | async-start | bytes 8388608
  155.6 7.6 %slice-start.2 = ((s8[9437184]{0:T(1024)(128)(4,1)}), s8[4194304]{0:T(1024)(128)(4,1)S(1)}, s32[]{:S(2)}) async-start(s8[9437184]{0:T(1024)(128)(4,1)} %bitcast.31), calls=%async_computation.4 | async-start | bytes 8388608
  160.8 2.5 %copy-start.12 = (bf16[704,1024]{1,0:T(8,128)(2,1)S(1)}, bf16[704,1024]{1,0:T(8,128)(2,1)}, u32[]{:S(2)}) copy-start(bf16[704,1024]{1,0:T(8,128)(2,1)} %get-tuple-element.22) | copy-start | bytes 4325380
  163.3 3.2 %copy-start.9 = (bf16[704,128]{1,0:T(8,128)(2,1)S(1)}, bf16[704,128]{1,0:T(8,128)(2,1)}, u32[]{:S(2)}) copy-start(bf16[704,128]{1,0:T(8,128)(2,1)} %get-tuple-element.23) | copy-start | bytes 540676
  166.5 2.5 %copy-start.11 = (bf16[704,1024]{1,0:T(8,128)(2,1)S(1)}, bf16[704,1024]{1,0:T(8,128)(2,1)}, u32[]{:S(2)}) copy-start(bf16[704,1024]{1,0:T(8,128)(2,1)} %get-tuple-element.24) | copy-start | bytes 4325380
  168.9 3.1 %copy-start.7 = (bf16[128,2048]{1,0:T(8,128)(2,1)S(1)}, bf16[128,2048]{1,0:T(8,128)(2,1)}, u32[]{:S(2)}) copy-start(bf16[128,2048]{1,0:T(8,128)(2,1)} %get-tuple-element.26) | copy-start | bytes 1572868
  168.9 3.2 %copy-start.8 = (bf16[704,128]{1,0:T(8,128)(2,1)S(1)}, bf16[704,128]{1,0:T(8,128)(2,1)}, u32[]{:S(2)}) copy-start(bf16[704,128]{1,0:T(8,128)(2,1)} %get-tuple-element.25) | copy-start | bytes 540676
  172.1 43.6 %copy-start.4 = (s32[64,6]{0,1:T(8,128)S(1)}, s32[64,6]{0,1:T(8,128)}, u32[]{:S(2)}) copy-start(s32[64,6]{0,1:T(8,128)} %param.10) | copy-start | bytes 4612
  172.1 43.6 %copy-start.5 = (bf16[64,6]{0,1:T(8,128)(2,1)S(1)}, bf16[64,6]{0,1:T(8,128)(2,1)}, u32[]{:S(2)}) copy-start(bf16[64,6]{0,1:T(8,128)(2,1)} %param.9) | copy-start | bytes 2308
